TPU v7x, 32 devices: a whole 2x2x4 slice. The times are simulated.
32 devices in a mesh: dp: 16 (over z, y, x), head: 2 (over core).
Axes of the slice: x: 2, y: 2, z: 4, core: 2. Of those that a mesh axis runs over, the one named last changes fastest.
Arguments:
- token_ids: int32 [16384], P(('dp', 'head')), may hold values from 0 to 30719, as said below
- lengths: int32 [32], P(('dp', 'head')), may hold values from 64 to 512, as said below
- embed_table: bfloat16 [30720, 768], P('dp', 'head'), as said below
- qkv_weight: bfloat16 [3, 768, 768], P(None, None, 'head'), as said below
- out_weight: bfloat16 [768, 768], replicated, as said below
- first_gain: float32 [768], replicated, may hold values from 0.25 to 1.75
- first_bias: float32 [768], replicated, may hold values from -3 to 3
- in_weight: bfloat16 [768, 3072], replicated, may hold values from -0.21875 to 0.21875
- back_weight: bfloat16 [3072, 768], replicated, may hold values from -0.109375 to 0.109375
- second_gain: float32 [768], replicated, may hold values from 0.25 to 1.75
- term_vector: float32 [768], replicated, may hold values from -0.21875 to 0.21875
- cotangent: float32 [16384], P(('dp', 'head')), may hold values from -6 to 6
Outputs:
- term_weights: float32 [16384], P(('dp', 'head'))
- grad_table: float32 [30720, 768], P('dp', 'head')
- grad_qkv: float32 [3, 768, 768], P(None, 'dp', 'head')
- grad_out: float32 [768, 768], P(None, ('dp', 'head'))
- grad_in: float32 [768, 3072], P(None, ('dp', 'head'))
- grad_back: float32 [3072, 768], P(('dp', 'head'))
- grad_first_gain: float32 [768], P(('dp', 'head'))
- grad_first_bias: float32 [768], P(('dp', 'head'))
- grad_second_gain: float32 [768], P(('dp', 'head'))
- grad_term_vector: float32 [768], P(('dp', 'head'))
Inputs may be any that keep to these rules, and one draw needn't show every extreme that they name: `token_ids`: in each aligned block of 1024 ids, at most 128 lie in any one range of 1920 rows that starts at a multiple of 1920, and some range holds exactly 128. `lengths`: some passage is full. `embed_table`: independent entries of deviation 1. `qkv_weight`: independent entries of deviation 1 / sqrt(768). `out_weight`: independent entries of deviation 1 / sqrt(6).
All inputs are finite; a program needn't handle non-finite values.
Results may differ from a plain program's by a relative error of at most 0.014.
Values may be sent and summed in bfloat16 or wider, within the bound.
No kernel may reach another device: no remote copies, remote signals or barrier semaphores. Data moves between devices by JAX's collectives and lax.ppermute only.
A program may use at most 128 MiB of HBM per device.

v0:
```python
import jax
import jax.numpy as jnp
from jax import lax
from jax.sharding import PartitionSpec as P

HDIM = 64
SEQ = 512


def layer_norm(values, norm_gain, norm_bias):
    centre = values - jnp.mean(values, -1, keepdims=True)
    spread = jnp.mean(centre * centre, -1, keepdims=True)
    return centre * lax.rsqrt(spread + 1e-12) * norm_gain + norm_bias


def gain_norm(values, norm_gain):
    centre = values - jnp.mean(values, -1, keepdims=True)
    spread = jnp.mean(centre * centre, -1, keepdims=True)
    return centre * lax.rsqrt(spread + 1e-12) * norm_gain


def gelu_exact(values):
    return jax.nn.gelu(values, approximate=False)


def body(
    token_ids,
    lengths,
    embed_table,
    qkv_weight,
    out_weight,
    first_gain,
    first_bias,
    in_weight,
    back_weight,
    second_gain,
    term_vector,
    cotangent,
):
    highest = lax.Precision.HIGHEST
    tok_rows = token_ids.shape[0]
    head_index = lax.axis_index("head")
    owner_count = lax.axis_size("dp")
    head_count = lax.axis_size("head")
    pair_rows = head_count * tok_rows
    capacity = 2 * pair_rows // owner_count
    block_rows = embed_table.shape[0]
    half_width = embed_table.shape[1]
    pair_ids, pair_lengths = (
        lax.all_gather(token_ids, "head", axis=0, tiled=True),
        lax.all_gather(lengths, "head", axis=0, tiled=True),
    )
    owner_of = pair_ids // block_rows
    offset = pair_ids - owner_of * block_rows
    owner_marks = (owner_of[:, None] == jnp.arange(owner_count, dtype=jnp.int32)[None, :]).astype(
        jnp.int32
    )
    before = jnp.cumsum(owner_marks, 0) - owner_marks
    rank_in = jnp.sum(before * owner_marks, 1)
    slot_of = owner_of * capacity + rank_in
    wanted = (
        jnp.full((owner_count * capacity,), -1, jnp.int32)
        .at[slot_of]
        .set(offset)
        .reshape(owner_count, capacity)
    )
    asked_rows = lax.all_to_all(wanted, "dp", split_axis=0, concat_axis=0, tiled=True)
    present = asked_rows >= 0
    asked_flat = jnp.maximum(asked_rows, 0).reshape(owner_count * capacity)
    picked = jnp.take(embed_table, asked_flat, axis=0).reshape(owner_count, capacity, half_width)
    picked = jnp.where(present[:, :, None], picked, jnp.zeros_like(picked))
    fetched = lax.all_to_all(picked, "dp", split_axis=0, concat_axis=0, tiled=True)
    half_rows = jnp.take(fetched.reshape(owner_count * capacity, half_width), slot_of, axis=0)
    embedded = lax.all_gather(half_rows, "head", axis=1, tiled=True)
    local_heads = qkv_weight.shape[2] // HDIM
    seq_count = pair_rows // SEQ
    projected = jnp.einsum(
        "td,cde->cte", embedded, qkv_weight, preferred_element_type=jnp.float32
    ).astype(jnp.bfloat16)
    shaped = projected.reshape(3, seq_count, SEQ, local_heads, HDIM)
    queries = shaped[0]
    key_rows = shaped[1]
    value_rows = shaped[2]
    key_live = jnp.arange(SEQ, dtype=jnp.int32)[None, :] < pair_lengths[:, None]
    raw_scores = (
        jnp.einsum("sqhd,skhd->shqk", queries, key_rows, preferred_element_type=jnp.float32) * 0.125
    )
    logits = jnp.where(key_live[:, None, None, :], raw_scores, -1e30)
    row_top = jnp.max(logits, -1, keepdims=True)
    powers = jnp.exp(logits - row_top)
    attn_probs = powers / jnp.sum(powers, -1, keepdims=True)
    attn_low = attn_probs.astype(jnp.bfloat16)
    attended = jnp.einsum(
        "shqk,skhd->sqhd", attn_low, value_rows, preferred_element_type=jnp.float32
    )
    attended = attended.astype(jnp.bfloat16).reshape(pair_rows, local_heads * HDIM)
    merged = lax.all_to_all(attended, "head", split_axis=0, concat_axis=1, tiled=True)
    own_rows = lax.dynamic_slice_in_dim(embedded, head_index * tok_rows, tok_rows, 0).astype(
        jnp.float32
    )
    branch = jnp.dot(merged, out_weight, preferred_element_type=jnp.float32)
    summed = own_rows + branch
    normed, first_back = jax.vjp(layer_norm, summed, first_gain, first_bias)
    normed_low = normed.astype(jnp.bfloat16)
    inner_pre = jnp.dot(normed_low, in_weight, preferred_element_type=jnp.float32)
    active, gelu_back = jax.vjp(gelu_exact, inner_pre)
    active_low = active.astype(jnp.bfloat16)
    outer_out = jnp.dot(active_low, back_weight, preferred_element_type=jnp.float32)
    final_rows, second_back = jax.vjp(gain_norm, normed + outer_out, second_gain)
    logit_rows = jnp.dot(final_rows, term_vector, precision=highest)
    positions = jnp.arange(tok_rows, dtype=jnp.int32) % SEQ
    live_mask = (positions < jnp.repeat(lengths, SEQ)).astype(jnp.float32)
    weights_out = jax.nn.softplus(logit_rows) * live_mask
    grad_logit = cotangent * live_mask * jax.nn.sigmoid(logit_rows)
    grad_term = jnp.dot(grad_logit, final_rows, precision=highest)
    grad_final = grad_logit[:, None] * term_vector[None, :]
    grad_mixed, grad_gain_two = second_back(grad_final)
    grad_outer = grad_mixed.astype(jnp.bfloat16)
    part_back = jnp.einsum("tf,td->fd", active_low, grad_outer, preferred_element_type=jnp.float32)
    grad_active = jnp.einsum(
        "td,fd->tf", grad_outer, back_weight, preferred_element_type=jnp.float32
    )
    (grad_inner,) = gelu_back(grad_active)
    grad_inner_low = grad_inner.astype(jnp.bfloat16)
    part_in = jnp.einsum(
        "td,tf->df", normed_low, grad_inner_low, preferred_element_type=jnp.float32
    )
    normed_term = jnp.einsum(
        "tf,df->td", grad_inner_low, in_weight, preferred_element_type=jnp.float32
    )
    grad_normed = grad_mixed + normed_term
    grad_summed, grad_gain_one, grad_bias_one = first_back(grad_normed)
    grad_branch = grad_summed.astype(jnp.bfloat16)
    part_out = jnp.einsum("te,td->ed", merged, grad_branch, preferred_element_type=jnp.float32)
    grad_merged = jnp.einsum(
        "td,ed->te", grad_branch, out_weight, preferred_element_type=jnp.float32
    ).astype(jnp.bfloat16)
    grad_attended = lax.all_to_all(grad_merged, "head", split_axis=1, concat_axis=0, tiled=True)
    grad_heads = grad_attended.reshape(seq_count, SEQ, local_heads, HDIM)
    grad_probs = jnp.einsum(
        "sqhd,skhd->shqk", grad_heads, value_rows, preferred_element_type=jnp.float32
    )
    grad_values = jnp.einsum(
        "shqk,sqhd->skhd", attn_low, grad_heads, preferred_element_type=jnp.float32
    )
    grad_raw = (
        attn_probs * (grad_probs - jnp.sum(attn_probs * grad_probs, -1, keepdims=True))
    ).astype(jnp.bfloat16)
    grad_queries = (
        jnp.einsum("shqk,skhd->sqhd", grad_raw, key_rows, preferred_element_type=jnp.float32)
        * 0.125
    )
    grad_keys = (
        jnp.einsum("shqk,sqhd->skhd", grad_raw, queries, preferred_element_type=jnp.float32) * 0.125
    )
    grad_proj = (
        jnp.stack([grad_queries, grad_keys, grad_values])
        .astype(jnp.bfloat16)
        .reshape(3, pair_rows, local_heads * HDIM)
    )
    part_qkv = jnp.einsum("td,cte->cde", embedded, grad_proj, preferred_element_type=jnp.float32)
    grad_embed = jnp.einsum(
        "cte,cde->td", grad_proj, qkv_weight, preferred_element_type=jnp.float32
    )
    own_part = (
        lax.dynamic_slice_in_dim(grad_embed, head_index * tok_rows, tok_rows, 0) + grad_summed
    )
    placed = lax.dynamic_update_slice_in_dim(grad_embed, own_part, head_index * tok_rows, 0)
    grad_half = lax.psum_scatter(
        placed.astype(jnp.bfloat16), "head", scatter_dimension=1, tiled=True
    ).astype(jnp.float32)
    send_rows = (
        jnp.zeros((owner_count * capacity, half_width), jnp.float32).at[slot_of].set(grad_half)
    )
    arrived = lax.all_to_all(
        send_rows.reshape(owner_count, capacity, half_width).astype(jnp.bfloat16),
        "dp",
        split_axis=0,
        concat_axis=0,
        tiled=True,
    ).astype(jnp.float32)
    arrived = jnp.where(present[:, :, None], arrived, 0.0).reshape(
        owner_count * capacity, half_width
    )
    grad_table = jnp.zeros((block_rows, half_width), jnp.float32).at[asked_flat].add(arrived)
    grad_qkv = lax.psum_scatter(part_qkv, "dp", scatter_dimension=1, tiled=True)
    summed_grads = (
        lax.psum_scatter(part_out, ("dp", "head"), scatter_dimension=1, tiled=True),
        lax.psum_scatter(part_in, ("dp", "head"), scatter_dimension=1, tiled=True),
        lax.psum_scatter(part_back, ("dp", "head"), scatter_dimension=0, tiled=True),
        lax.psum_scatter(grad_gain_one, ("dp", "head"), scatter_dimension=0, tiled=True),
        lax.psum_scatter(grad_bias_one, ("dp", "head"), scatter_dimension=0, tiled=True),
        lax.psum_scatter(grad_gain_two, ("dp", "head"), scatter_dimension=0, tiled=True),
        lax.psum_scatter(grad_term, ("dp", "head"), scatter_dimension=0, tiled=True),
    )
    return (
        weights_out,
        grad_table,
        grad_qkv,
        summed_grads[0],
        summed_grads[1],
        summed_grads[2],
        summed_grads[3],
        summed_grads[4],
        summed_grads[5],
        summed_grads[6],
    )


def solution(mesh):
    in_specs = (
        P(("dp", "head")),
        P(("dp", "head")),
        P("dp", "head"),
        P(None, None, "head"),
        P(),
        P(),
        P(),
        P(),
        P(),
        P(),
        P(),
        P(("dp", "head")),
    )
    out_specs = (
        P(("dp", "head")),
        P("dp", "head"),
        P(None, "dp", "head"),
        P(None, ("dp", "head")),
        P(None, ("dp", "head")),
        P(("dp", "head"), None),
        P(("dp", "head")),
        P(("dp", "head")),
        P(("dp", "head")),
        P(("dp", "head")),
    )
    return jax.shard_map(body, mesh=mesh, in_specs=in_specs, out_specs=out_specs, check_vma=False)
```

profile of v0, /device:TPU:0, one launch (start us, length us, event | category | flops | bytes accessed | tf_op | source)
XLA Modules:
  0.0 857.9 jit_solution(12759508367868988017)
XLA Ops:
  18.7 15.2 %all_to_all.54 = s32[16,1,128]{2,1,0:T(1,128)S(1)} all-to-all(s32[16,1,128]{2,1,0:T(1,128)S(1)} %bitcast.129), channel_id=1, replica_groups=mesh['dp'=16,'head'=2] {'dp'}, dimensions={0} | all-to-all | bytes 16384 | tf_op jit(solution)/shard_map/all_to_all | solution.py:67
  34.6 8.8 %gather_fusion = bf16[2048,384]{1,0:T(8,128)(2,1)S(1)} fusion(bf16[1920,384]{1,0:T(8,128)(2,1)} %param.14, s32[2048]{0:T(1024)S(1)} %broadcast_clamp_fusion), kind=kCustom, calls=%fused_computation | custom fusion | bytes 3153920 | tf_op jit(solution)/shard_map/jit(_take)/gather | solution.py:70
  48.8 33.6 %all-to-all-done.1 = bf16[16,128,384]{2,1,0:T(8,128)(2,1)S(1)} async-done(((bf16[16,128,384]{2,1,0:T(8,128)(2,1)}), bf16[16,128,384]{2,1,0:T(8,128)(2,1)S(1)}, u32[]{:S(2)}, u32[]{:S(2)}) %all-to-all-start.1) | async-done | bytes 1572896 | tf_op jit(solution)/shard_map/all_to_all | solution.py:72
  82.3 5.0 gather_fusion.1
  93.5 7.6 all-gather.3.cloned.1.call-done
  116.9 11.0 %fusion.103 = (f32[2,6,512]{2,1,0:T(8,128)S(1)}, f32[2,6,512,512]{2,3,1,0:T(8,128)}) fusion(pred[2,512]{1,0:T(4,128)(4,1)S(1)} %iota_compare_fusion.2, bf16[2,512,6,64]{1,0,3,2:T(2,128)(2,1)} %squeeze.11, bf16[2,512,6,64]{1,0,3,2:T(2,128)(2,1)} %squeeze.10), kind=kOutput, calls=%fused_computation.161 | convolution fusion | flops 415236608 | bytes 14181376 | tf_op jit(solution)/shard_map/sub | solution.py:90
  127.9 5.9 fusion.30
  140.0 20.0 %multiply_convert_fusion.1 = (bf16[512,3072]{1,0:T(8,128)(2,1)S(1)}, f32[512,3072]{1,0:T(8,128)}, f32[512,3072]{1,0:T(8,128)}) fusion(bf16[768,3072]{1,0:T(8,128)(2,1)} %param.19, f32[512,768]{1,0:T(8,128)S(1)} %get-tuple-element.78, f32[768]{0:T(1024)S(1)} %copy-done.20, f32[768]{0:T(1024)S(1)} %copy-done.16, f32[512]{0:T(512)S(1)} %fusion.85, ...), kind=kOutput, calls=%fused_computation.14 | convolution fusion | flops 2520121344 | bytes 22030336 | tf_op jit(solution)/shard_map/dot_general | solution.py:105
  166.8 7.3 add_convert_fusion
  179.3 5.3 all_to_all.56
  187.0 12.0 %multiply_reduce_fusion = (f32[2,6,512]{2,1,0:T(8,128)S(1)}, f32[2,6,512,512]{2,3,1,0:T(8,128)}) fusion(f32[2,6,512,512]{2,3,1,0:T(8,128)} %get-tuple-element.76, f32[2,6,512]{2,1,0:T(8,128)S(1)} %get-tuple-element.75, bf16[2,512,6,64]{1,3,2,0:T(8,128)(2,1)} %bitcast.118, bf16[2,512,6,64]{1,0,3,2:T(2,128)(2,1)} %copy-done.7), kind=kOutput, calls=%fused_computation.7 | convolution fusion | flops 412084224 | bytes 26787840 | tf_op jit(solution)/shard_map/sqhd,skhd->shqk/dot_general | solution.py:140
  199.0 6.8 multiply_convert_fusion
  245.2 6.0 convolution_bitcast_fusion
  251.2 6.3 copy.113
  261.6 9.2 %fusion.92 = f32[3072,768]{1,0:T(8,128)} fusion(bf16[512,3072]{1,0:T(8,128)(2,1)} %copy-done.24, f32[512]{0:T(512)S(1)} %negate_multiply_fusion.2, f32[512,768]{1,0:T(8,128)S(1)} %get-tuple-element.81, f32[512]{0:T(512)S(1)} %multiply_multiply_fusion.8, f32[768]{0:T(1024)S(1)} %copy-done.12, f32[512]{0:T(512)S(1)} %get-tuple-element.73, ...), kind=kOutput, calls=%fused_computation.153 | convolution fusion | flops 2419458048 | bytes 14172160 | tf_op jit(solution)/shard_map/tf,td->fd/dot_general | solution.py:119
  271.1 8.8 %fusion.95 = f32[768,3072]{0,1:T(8,128)} fusion(bf16[512,3072]{1,0:T(8,128)(2,1)} %copy-done.23, f32[512,768]{1,0:T(8,128)} %copy-done.3, f32[768]{0:T(1024)S(1)} %copy-done.20, f32[768]{0:T(1024)S(1)} %copy-done.16, f32[512]{0:T(512)S(1)} %fusion.85, f32[512]{0:T(512)S(1)} %broadcast_multiply_fusion.1), kind=kOutput, calls=%fused_computation.156 | convolution fusion | flops 2417885184 | bytes 14166016 | tf_op jit(solution)/shard_map/td,tf->df/dot_general | solution.py:125
  282.2 7.2 scatter_custom_fusion.1
  292.7 7.0 all-to-all-start.4
  302.1 71.5 %all-reduce.6 = (f32[768]{0:T(1024)S(1)}, f32[768]{0:T(1024)S(1)}, f32[768]{0:T(1024)S(1)}, f32[768]{0:T(1024)S(1)}) all-reduce(f32[768]{0:T(1024)S(1)} %get-tuple-element.50, f32[768]{0:T(1024)S(1)} %get-tuple-element.54, f32[768]{0:T(1024)S(1)} %get-tuple-element.52, ...), channel_id=7, replica_groups=mesh['dp'=16,'head'=2] {'dp','head'}, use_global_device_ids=true, to_apply=%region_23.24.clone | all-reduce | flops 3072 | bytes 24576
  376.0 87.9 %all-reduce.9.cloned.1.call-done = f32[3,768,384]{2,0,1:T(4,128)} async-done(((f32[3,768,384]{2,0,1:T(4,128)}), f32[3,768,384]{2,0,1:T(4,128)}) %all-reduce.9.cloned.1.call-update) | async-done | bytes 3538960
  468.7 15.8 %scatter_custom_fusion.2 = f32[1920,384]{1,0:T(8,128)} fusion(s32[2048]{0:T(1024)S(1)} %maximum_bitcast_fusion, f32[2048,384]{1,0:T(8,128)} %bitcast.114, f32[]{:T(128)} %constant.68.clone.1), kind=kCustom, calls=%fused_computation.71 | custom fusion | flops 786432 | bytes 2949632 | tf_op jit(solution)/shard_map/scatter-add | solution.py:185
  484.5 83.2 %reduce-scatter.7.cloned.1.call-done = f32[768,24]{0,1:T(8,128)} async-done(((f32[768,768]{0,1:T(8,128)}), f32[768,24]{0,1:T(8,128)}) %reduce-scatter.7.cloned.1.call-update) | async-done | bytes 73744 | tf_op jit(solution)/shard_map/reduce_scatter | solution.py:188
  567.7 142.0 %reduce-scatter.11.cloned.1.call-done = f32[96,768]{1,0:T(8,128)} async-done(((f32[3072,768]{1,0:T(8,128)}), f32[96,768]{1,0:T(8,128)}) %reduce-scatter.11.cloned.1.call-update) | async-done | bytes 294928 | tf_op jit(solution)/shard_map/reduce_scatter | solution.py:190
  709.7 140.9 %reduce-scatter.9.cloned.1.call-done = f32[768,96]{0,1:T(8,128)} async-done(((f32[768,3072]{0,1:T(8,128)}), f32[768,96]{0,1:T(8,128)}) %reduce-scatter.9.cloned.1.call-update) | async-done | bytes 294928 | tf_op jit(solution)/shard_map/reduce_scatter | solution.py:189
  (165 shorter events, 116.9 us)
Async XLA Ops:
  7.2 94.0 %copy-start = (bf16[3,768,384]{2,1,0:T(8,128)(2,1)S(1)}, bf16[3,768,384]{2,1,0:T(8,128)(2,1)}, u32[]{:S(2)}) copy-start(bf16[3,768,384]{2,1,0:T(8,128)(2,1)} %param.15) | copy-start | bytes 5308420
  14.4 34.3 %copy-start.15 = (s32[1024]{0:T(1024)}, s32[1024]{0:T(1024)S(1)}, u32[]{:S(2)}) copy-start(s32[1024]{0:T(1024)S(1)} %get-tuple-element.64) | copy-start | bytes 12292
  34.6 8.8 %copy-start.13 = (pred[16,128]{1,0:T(8,128)(4,1)}, pred[16,128]{1,0:T(8,128)(4,1)S(1)}, u32[]{:S(2)}) copy-start(pred[16,128]{1,0:T(8,128)(4,1)S(1)} %get-tuple-element.68) | copy-start | bytes 6148
  45.0 37.3 %all-to-all-start.1 = ((bf16[16,128,384]{2,1,0:T(8,128)(2,1)}), bf16[16,128,384]{2,1,0:T(8,128)(2,1)S(1)}, u32[]{:S(2)}, u32[]{:S(2)}) async-start(bf16[16,128,384]{2,1,0:T(8,128)(2,1)} %select_select_fusion), calls=%async_computation.1 | async-start | bytes 3145728 | tf_op jit(solution)/shard_map/all_to_all | solution.py:72
  48.7 52.5 %all-gather.3.cloned.1.call-start = ((), (), s32[]{:S(2)}) async-start(), calls=%async_computation.9 | async-start | bytes 2359296 | tf_op jit(solution)/shard_map/all_gather | solution.py:74
  89.6 190.3 %reduce-scatter.13.cloned.1.call-start = ((), (), s32[]{:S(2)}) async-start(), calls=%async_computation.13 | async-start | bytes 2359296
  116.9 11.0 %copy-start.7 = (bf16[2,512,6,64]{1,0,3,2:T(2,128)(2,1)}, bf16[2,512,6,64]{1,0,3,2:T(2,128)(2,1)S(1)}, u32[]{:S(2)}) copy-start(bf16[2,512,6,64]{1,0,3,2:T(2,128)(2,1)S(1)} %squeeze.9) | copy-start | bytes 2359300
  127.9 10.8 %copy-start.18 = (bf16[1024,768]{1,0:T(8,128)(2,1)S(1)}, bf16[1024,768]{1,0:T(8,128)(2,1)}, u32[]{:S(2)}) copy-start(bf16[1024,768]{1,0:T(8,128)(2,1)} %all-gather.3.cloned.1.call-done) | copy-start | bytes 4718596
  127.9 10.8 %copy-start.19 = (bf16[768,768]{1,0:T(8,128)(2,1)S(1)}, bf16[768,768]{1,0:T(8,128)(2,1)}, u32[]{:S(2)}) copy-start(bf16[768,768]{1,0:T(8,128)(2,1)} %param.16) | copy-start | bytes 3538948
  138.7 21.3 %slice-start.3 = ((s8[4718592]{0:T(1024)(128)(4,1)}), s8[4194304]{0:T(1024)(128)(4,1)S(1)}, s32[]{:S(2)}) async-start(s8[4718592]{0:T(1024)(128)(4,1)} %bitcast.133), calls=%async_computation.18 | async-start | bytes 8388608
  139.6 37.9 %copy-start.3 = (f32[512,768]{1,0:T(8,128)}, f32[512,768]{1,0:T(8,128)S(1)}, u32[]{:S(2)}) copy-start(f32[512,768]{1,0:T(8,128)S(1)} %get-tuple-element.78) | copy-start | bytes 4718596
  140.0 20.1 %slice-start.4 = ((s8[4718592]{0:T(1024)(128)(4,1)}), s8[524288]{0:T(1024)(128)(4,1)S(1)}, s32[]{:S(2)}) async-start(s8[4718592]{0:T(1024)(128)(4,1)} %bitcast.133), calls=%async_computation.19 | async-start | bytes 1048576
  163.2 11.0 %slice-start.5 = ((s8[4718592]{0:T(1024)(128)(4,1)}), s8[4194304]{0:T(1024)(128)(4,1)S(1)}, s32[]{:S(2)}) async-start(s8[4718592]{0:T(1024)(128)(4,1)} %bitcast.135), calls=%async_computation.20 | async-start | bytes 8388608
  166.8 7.4 slice-start.6
  187.0 12.0 %slice-start = ((s8[12582912]{0:T(1024)(128)(4,1)}), s8[4194304]{0:T(1024)(128)(4,1)S(1)}, s32[]{:S(2)}) async-start(s8[12582912]{0:T(1024)(128)(4,1)} %bitcast.107), calls=%async_computation.15 | async-start | bytes 8388608
  187.0 12.0 %slice-start.1 = ((s8[12582912]{0:T(1024)(128)(4,1)}), s8[4194304]{0:T(1024)(128)(4,1)S(1)}, s32[]{:S(2)}) async-start(s8[12582912]{0:T(1024)(128)(4,1)} %bitcast.107), calls=%async_computation.16 | async-start | bytes 8388608
  187.0 12.0 %slice-start.2 = ((s8[12582912]{0:T(1024)(128)(4,1)}), s8[4194304]{0:T(1024)(128)(4,1)S(1)}, s32[]{:S(2)}) async-start(s8[12582912]{0:T(1024)(128)(4,1)} %bitcast.107), calls=%async_computation.17 | async-start | bytes 8388608
  245.1 218.8 %all-reduce.9.cloned.1.call-start = ((), (), s32[]{:S(2)}) async-start(), calls=%async_computation.14 | async-start | bytes 9437184
  257.5 310.2 %reduce-scatter.7.cloned.1.call-start = ((), (), s32[]{:S(2)}) async-start(), calls=%async_computation.10 | async-start | bytes 2433024 | tf_op jit(solution)/shard_map/reduce_scatter | solution.py:188
  261.5 448.2 %reduce-scatter.11.cloned.1.call-start = ((), (), s32[]{:S(2)}) async-start(), calls=%async_computation.12 | async-start | bytes 9732096 | tf_op jit(solution)/shard_map/reduce_scatter | solution.py:190
  270.8 579.8 %reduce-scatter.9.cloned.1.call-start = ((), (), s32[]{:S(2)}) async-start(), calls=%async_computation.11 | async-start | bytes 9732096 | tf_op jit(solution)/shard_map/reduce_scatter | solution.py:189
  292.7 8.3 copy-start.10
  292.7 172.9 %copy-start.14 = (pred[16,128]{1,0:T(8,128)(4,1)S(1)}, pred[16,128]{1,0:T(8,128)(4,1)}, u32[]{:S(2)}) copy-start(pred[16,128]{1,0:T(8,128)(4,1)} %copy-done.13) | copy-start | bytes 6148
  292.7 172.9 %all-to-all-start.4 = ((bf16[16,128,384]{2,1,0:T(8,128)(2,1)}), bf16[16,128,384]{2,1,0:T(8,128)(2,1)}, u32[]{:S(2)}, u32[]{:S(2)}) async-start(bf16[16,128,384]{2,1,0:T(8,128)(2,1)} %bitcast.111), calls=%async_computation.4 | async-start | bytes 3145728 | tf_op jit(solution)/shard_map/all_to_all | solution.py:175
  (16 other events, 47.8 us)
Sparse Core Ops, SparseCore 0:
  89.7 11.3 all-gather.2
  245.3 10.2 reduce-scatter.12
  262.2 201.6 all-reduce.8
  469.6 98.0 reduce-scatter.6
  575.0 134.6 reduce-scatter.10
  716.0 134.5 reduce-scatter.8
where the time goes:
time: 864 us; the launch traced here: 858 us
  waiting for transfers between devices  495 us (57%)
  matrix products  109 us (13%)
  blocking collectives  101 us (12%)
  local copies, waits for them, and re-layouts  75 us (9%)
  other arithmetic  49.6 us (6%)
  between operations  16.4 us (2%)
  starting transfers between devices  11.2 us (1%)
    reduce_scatter x1, waiting for transfers between devices, body(): lax.psum_scatter(part_back, ('dp', 'head'), scatter_dimension=0, tiled=True)  142 us
    reduce_scatter x1, waiting for transfers between devices, body(): lax.psum_scatter(part_in, ('dp', 'head'), scatter_dimension=1, tiled=True)  141 us
    unnamed x8, waiting for transfers between devices  88 us
    reduce_scatter x1, waiting for transfers between devices, body(): lax.psum_scatter(part_out, ('dp', 'head'), scatter_dimension=1, tiled=True)  83.2 us
    unnamed x2, blocking collectives  73.4 us
    all_to_all x1, waiting for transfers between devices, body(): lax.all_to_all(picked, 'dp', split_axis=0, concat_axis=0, tiled=True)  33.6 us
    dot_general x1, matrix products, body(): jnp.dot(normed_low, in_weight, preferred_element_type=jnp.float32)  20 us
  transfers between devices with their start and end apart: 8, of which 6 were waited for; matrix products, arithmetic and copies ran while one was open for 9% of the time, Pallas kernels for 0%

commit v1 on v0

v1 whole, which is shorter than its diff:
```python
import functools

import jax
import jax.numpy as jnp
from jax import lax
from jax.experimental import pallas as pl
from jax.experimental.pallas import tpu as pltpu
from jax.sharding import PartitionSpec as P

HDIM = 64
LOG2E = 1.4426950408889634
BF = jnp.bfloat16
F32 = jnp.float32
VMEM_LIMIT = 48 * 1024 * 1024


def dot_nn(a, b):
    return lax.dot_general(a, b, (((1,), (0,)), ((), ())), preferred_element_type=F32)


def dot_nt(a, b):
    return lax.dot_general(a, b, (((1,), (1,)), ((), ())), preferred_element_type=F32)


def dot_tn(a, b):
    return lax.dot_general(a, b, (((0,), (0,)), ((), ())), preferred_element_type=F32)


def iota(shape, dim):
    return lax.broadcasted_iota(jnp.int32, shape, dim)


def params(**more):
    return pltpu.CompilerParams(vmem_limit_bytes=VMEM_LIMIT, **more)


def whole(shape):
    return pl.BlockSpec(shape, lambda *_: (0,) * len(shape))


def cost(flops, moved, trans=0):
    return pl.CostEstimate(flops=int(flops), bytes_accessed=int(moved), transcendentals=int(trans))


def pick_kernel(place, ids_ref, table_ref, picked_ref, asked_ref, row_ref, col_ref, rank_s, hi_s, lo_s, hot_s):
    owners, block = ids_ref.shape
    rows = table_ref.shape[0]
    cap = picked_ref.shape[0] // owners
    dp = place[0]
    ids = ids_ref[...]
    away = ids - dp * rows
    mine = (away >= 0) & (away < rows)
    floor = iota((owners, block), 0) * rows
    own_ids = ids_ref[0:1, :]
    marks = (own_ids >= floor) & (own_ids < floor + rows)
    both = jnp.concatenate([mine.astype(F32), marks.astype(F32)], axis=0).astype(BF)
    upto = (iota((block, block), 0) <= iota((block, block), 1)).astype(F32).astype(BF)
    counts = dot_nn(both, upto)
    rank_s[...] = jnp.where(mine, counts[:owners], 0.0) - 1.0
    hi_s[...] = (away >> 6).astype(F32)
    lo_s[...] = (away & 63).astype(F32)
    spot = jnp.where(marks, counts[owners:] - 1.0 + iota((owners, block), 0).astype(F32) * cap, 0.0)
    slot = jnp.sum(spot, axis=0, keepdims=True)
    row_ref[...] = jnp.broadcast_to(slot, row_ref.shape)
    col_ref[...] = jnp.transpose(jnp.broadcast_to(slot, (128, block)))
    group = hot_s.shape[0] // cap

    def per_group(g, _):
        def per_block(i, _):
            j = g * group + i
            r = j ^ dp
            rank = rank_s[pl.ds(r, 1), :].astype(jnp.int32)
            sel = (iota((cap, block), 0) == rank).astype(F32).astype(BF)
            lane = iota((16, block), 0)
            code = jnp.where(lane == 0, hi_s[pl.ds(r, 1), :], jnp.where(lane == 1, lo_s[pl.ds(r, 1), :], 0.0)).astype(BF)
            cols = dot_nt(sel, code)
            asked_col = (cols[:, 0:1] * 64.0 + cols[:, 1:2]).astype(jnp.int32)
            lines = dot_nt(code, sel)
            asked_ref[pl.ds(j, 1), :] = lines[0:1, :] * 64.0 + lines[1:2, :]
            hot = (iota((cap, rows), 1) == asked_col).astype(F32).astype(BF)
            hot_s[pl.ds(pl.multiple_of(i * cap, cap), cap), :] = hot
            return 0

        lax.fori_loop(0, group, per_block, 0)
        size = group * cap
        picked_ref[pl.ds(pl.multiple_of(g * size, size), size), :] = dot_nn(hot_s[...], table_ref[...]).astype(BF)
        return 0

    lax.fori_loop(0, owners // group, per_group, 0)


def pick(dp, ids, table, cap):
    owners, block = ids.shape
    rows, half = table.shape
    group = min(owners, max(1, 512 // cap))
    shapes = (
        jax.ShapeDtypeStruct((owners * cap, half), BF),
        jax.ShapeDtypeStruct((owners, cap), F32),
        jax.ShapeDtypeStruct((8, block), F32),
        jax.ShapeDtypeStruct((block, 128), F32),
    )
    return pl.pallas_call(
        pick_kernel,
        grid_spec=pltpu.PrefetchScalarGridSpec(
            num_scalar_prefetch=1,
            grid=(1,),
            in_specs=[whole(ids.shape), whole(table.shape)],
            out_specs=[whole(s.shape) for s in shapes],
            scratch_shapes=[pltpu.VMEM((owners, block), F32)] * 3 + [pltpu.VMEM((group * cap, rows), BF)],
        ),
        out_shape=shapes,
        compiler_params=params(),
        name="pick",
    )(dp, ids, table)


def regather_kernel(col_ref, got_ref, own_ref, send_ref):
    slots = got_ref.shape[0]
    half = own_ref.shape[0]
    for part, out in ((1, send_ref), (0, own_ref)):
        slot = col_ref[part * half : (part + 1) * half, 0:1].astype(jnp.int32)
        hot = (iota((half, slots), 1) == slot).astype(F32).astype(BF)
        out[...] = dot_nn(hot, got_ref[...]).astype(BF)


def regather(col, got):
    block, half = col.shape[0], got.shape[1]
    shapes = [jax.ShapeDtypeStruct((block // 2, half), BF)] * 2
    return pl.pallas_call(
        regather_kernel,
        grid=(1,),
        in_specs=[whole(col.shape), whole(got.shape)],
        out_specs=[whole(s.shape) for s in shapes],
        out_shape=shapes,
        compiler_params=params(),
        name="regather",
    )(col, got)


def spread_kernel(row_ref, own_ref, other_ref, out_ref):
    half = own_ref.shape[0]
    step = out_ref.shape[0]
    base = pl.program_id(0) * step
    slot = row_ref[0:1, :].astype(jnp.int32)
    place = iota((step, half), 0) + base
    hot_own = (place == slot[:, :half]).astype(F32).astype(BF)
    hot_other = (place == slot[:, half:]).astype(F32).astype(BF)
    out_ref[...] = (dot_nn(hot_own, own_ref[...]) + dot_nn(hot_other, other_ref[...])).astype(BF)


def spread(row, own, other, slots):
    step = 512
    return pl.pallas_call(
        spread_kernel,
        grid=(slots // step,),
        in_specs=[whole(row.shape), whole(own.shape), whole(other.shape)],
        out_specs=pl.BlockSpec((step, own.shape[1]), lambda i: (i, 0)),
        out_shape=jax.ShapeDtypeStruct((slots, own.shape[1]), BF),
        compiler_params=params(),
        name="spread",
    )(row, own, other)


def table_kernel(asked_ref, got_ref, out_ref):
    step = out_ref.shape[0]
    base = pl.program_id(0) * step
    total = jnp.zeros(out_ref.shape, F32)
    lines, width = asked_ref.shape
    for c in range(lines):
        asked = asked_ref[c : c + 1, :].astype(jnp.int32)
        hot = (iota((step, width), 0) + base == asked).astype(F32).astype(BF)
        total = total + dot_nn(hot, got_ref[c * width : (c + 1) * width, :])
    out_ref[...] = total


def table_grad(asked, got, rows):
    step = 640 if rows % 640 == 0 else rows
    return pl.pallas_call(
        table_kernel,
        grid=(rows // step,),
        in_specs=[whole(asked.shape), whole(got.shape)],
        out_specs=pl.BlockSpec((step, got.shape[1]), lambda i: (i, 0)),
        out_shape=jax.ShapeDtypeStruct((rows, got.shape[1]), F32),
        compiler_params=params(),
        name="table_grad",
    )(asked, got)


def attend_kernel(place, own_ref, other_ref, weight_ref, emb_ref, proj_ref, out_ref, stat_ref):
    half = own_ref.shape[1]
    length = place[1]

    @pl.when(pl.program_id(0) == 0)
    def _():
        @pl.when(place[0] == 0)
        def _():
            emb_ref[:, :half] = own_ref[...]
            emb_ref[:, half:] = other_ref[...]

        @pl.when(place[0] != 0)
        def _():
            emb_ref[:, :half] = other_ref[...]
            emb_ref[:, half:] = own_ref[...]

    emb = emb_ref[...]
    seq = emb.shape[0]
    query = dot_nn(emb, weight_ref[0]).astype(BF)
    key = dot_nn(emb, weight_ref[1]).astype(BF)
    value = dot_nn(emb, weight_ref[2]).astype(BF)
    proj_ref[0] = query
    proj_ref[1] = key
    proj_ref[2] = value
    lane = iota(query.shape, 1)
    live = iota((seq, seq), 0) < length
    value_t = jnp.transpose(value)
    parts = []
    for h in range(2):
        this = (lane < HDIM) if h == 0 else (lane >= HDIM)
        masked = jnp.where(this, query, jnp.zeros_like(query))
        score = jnp.where(live, dot_nt(key, masked) * (0.125 * LOG2E), -1e30)
        top = jnp.max(score, axis=0, keepdims=True)
        power = jnp.exp2(score - top)
        total = jnp.sum(power, axis=0, keepdims=True)
        share = 1.0 / total
        stat_ref[0, 2 * h : 2 * h + 1, :] = top
        stat_ref[0, 2 * h + 1 : 2 * h + 2, :] = share
        low = (power * share).astype(BF)
        parts.append(dot_nn(value_t, low))
    picked = jnp.where(iota(parts[0].shape, 0) < HDIM, parts[0], parts[1])
    out_ref[...] = jnp.transpose(picked).astype(BF)


def attend(place, own, other, weight):
    seq, half = own.shape
    width = 2 * half
    pairs = width // 128
    shapes = (
        jax.ShapeDtypeStruct((seq, width), BF),
        jax.ShapeDtypeStruct((3, seq, width), BF),
        jax.ShapeDtypeStruct((seq, width), BF),
        jax.ShapeDtypeStruct((pairs, 8, seq), F32),
    )
    return pl.pallas_call(
        attend_kernel,
        grid_spec=pltpu.PrefetchScalarGridSpec(
            num_scalar_prefetch=1,
            grid=(pairs,),
            in_specs=[
                whole(own.shape),
                whole(other.shape),
                pl.BlockSpec((3, width, 128), lambda i, s: (0, 0, i)),
            ],
            out_specs=[
                whole((seq, width)),
                pl.BlockSpec((3, seq, 128), lambda i, s: (0, 0, i)),
                pl.BlockSpec((seq, 128), lambda i, s: (0, i)),
                pl.BlockSpec((1, 8, seq), lambda i, s: (i, 0, 0)),
            ],
        ),
        out_shape=shapes,
        compiler_params=params(),
        name="attend",
    )(place, own, other, weight)


def attend_back_kernel(place, proj_ref, grad_ref, stat_ref, weight_ref, sum_ref, gproj_ref, own_ref, send_ref, total_s):
    step = pl.program_id(0)
    length = place[1]
    query, key, value = proj_ref[0], proj_ref[1], proj_ref[2]
    grad = grad_ref[...]
    seq = grad.shape[0]
    lane = iota(query.shape, 1)
    live = iota((seq, seq), 0) < length
    key_t = jnp.transpose(key)
    outs = []
    for h in range(2):
        this = (lane < HDIM) if h == 0 else (lane >= HDIM)
        masked = jnp.where(this, query, jnp.zeros_like(query))
        grad_h = jnp.where(this, grad, jnp.zeros_like(grad))
        score = jnp.where(live, dot_nt(key, masked) * (0.125 * LOG2E), -1e30)
        probs = jnp.exp2(score - stat_ref[0, 2 * h : 2 * h + 1, :]) * stat_ref[0, 2 * h + 1 : 2 * h + 2, :]
        grad_value = dot_nn(probs.astype(BF), grad)
        grad_probs = dot_nt(value, grad_h)
        both = probs * grad_probs
        dots = jnp.sum(both, axis=0, keepdims=True)
        grad_raw = (both - probs * dots).astype(BF)
        grad_key = dot_nn(grad_raw, query) * 0.125
        grad_query_t = dot_nn(key_t, grad_raw) * 0.125
        outs.append((grad_query_t, grad_key, grad_value))
    grad_query = jnp.transpose(jnp.where(iota(outs[0][0].shape, 0) < HDIM, outs[0][0], outs[1][0])).astype(BF)
    grad_key = jnp.where(lane < HDIM, outs[0][1], outs[1][1]).astype(BF)
    grad_value = jnp.where(lane < HDIM, outs[0][2], outs[1][2]).astype(BF)
    gproj_ref[0] = grad_query
    gproj_ref[1] = grad_key
    gproj_ref[2] = grad_value
    more = dot_nt(grad_query, weight_ref[0]) + dot_nt(grad_key, weight_ref[1]) + dot_nt(grad_value, weight_ref[2])

    @pl.when(step == 0)
    def _():
        total_s[...] = sum_ref[...] + more

    @pl.when(step > 0)
    def _():
        total_s[...] += more

    @pl.when(step == pl.num_programs(0) - 1)
    def _():
        half = own_ref.shape[1]
        low = total_s[...].astype(BF)

        @pl.when(place[0] == 0)
        def _():
            own_ref[...] = low[:, :half]
            send_ref[...] = low[:, half:]

        @pl.when(place[0] != 0)
        def _():
            own_ref[...] = low[:, half:]
            send_ref[...] = low[:, :half]


def attend_back(place, proj, grad, stat, weight, grad_sum):
    seq, width = grad.shape
    pairs = width // 128
    shapes = (
        jax.ShapeDtypeStruct((3, seq, width), BF),
        jax.ShapeDtypeStruct((seq, width // 2), BF),
        jax.ShapeDtypeStruct((seq, width // 2), BF),
    )
    return pl.pallas_call(
        attend_back_kernel,
        grid_spec=pltpu.PrefetchScalarGridSpec(
            num_scalar_prefetch=1,
            grid=(pairs,),
            in_specs=[
                pl.BlockSpec((3, seq, 128), lambda i, s: (0, 0, i)),
                pl.BlockSpec((seq, 128), lambda i, s: (0, i)),
                pl.BlockSpec((1, 8, seq), lambda i, s: (i, 0, 0)),
                pl.BlockSpec((3, width, 128), lambda i, s: (0, 0, i)),
                whole((seq, width)),
            ],
            out_specs=[
                pl.BlockSpec((3, seq, 128), lambda i, s: (0, 0, i)),
                whole((seq, width // 2)),
                whole((seq, width // 2)),
            ],
            scratch_shapes=[pltpu.VMEM((seq, width), F32)],
        ),
        out_shape=shapes,
        compiler_params=params(),
        name="attend_back",
    )(place, proj, grad, stat, weight, grad_sum)


def gelu_parts(x):
    size = jnp.abs(x)
    t = 1.0 / (1.0 + (0.3275911 * 0.7071067811865476) * size)
    bell = jnp.exp2(x * x * (-0.5 * LOG2E))
    poly = t * (0.254829592 + t * (-0.284496736 + t * (1.421413741 + t * (-1.453152027 + t * 1.061405429))))
    tail = 0.5 * poly * bell
    phi_sum = jnp.where(x >= 0, 1.0 - tail, tail)
    return x * phi_sum, phi_sum + x * bell * 0.3989422804014327


def norm_parts(v):
    centre = v - jnp.mean(v, axis=-1, keepdims=True)
    spread_of = jnp.mean(centre * centre, axis=-1, keepdims=True)
    scale = lax.rsqrt(spread_of + 1e-12)
    return centre * scale, scale


def norm_back(grad, normal, scale, gain):
    e = grad * gain
    return scale * (e - jnp.mean(e, -1, keepdims=True) - normal * jnp.mean(e * normal, -1, keepdims=True))


def forward_kernel(
    place, att_ref, emb_ref, out_w_ref, vec_ref, cot_ref, in_ref, back_ref,
    low_ref, normal_ref, scale_ref, active_ref, slope_ref, mixed_ref, outer_ref, weights_ref, sums_ref,
):
    step = pl.program_id(0)
    seq = att_ref.shape[0]

    @pl.when(step == 0)
    def _():
        total = emb_ref[...].astype(F32) + dot_nn(att_ref[...], out_w_ref[...])
        normal, scale = norm_parts(total)
        normed = normal * vec_ref[0:1, :] + vec_ref[1:2, :]
        normal_ref[...] = normal
        scale_ref[...] = jnp.broadcast_to(scale, scale_ref.shape)
        low_ref[...] = normed.astype(BF)
        mixed_ref[...] = normed

    inner = dot_nt(low_ref[...], in_ref[...])
    active, slope = gelu_parts(inner)
    active = active.astype(BF)
    active_ref[...] = active
    slope_ref[...] = slope
    mixed_ref[...] += dot_nn(active, back_ref[...])

    @pl.when(step == pl.num_programs(0) - 1)
    def _():
        normal, scale = norm_parts(mixed_ref[...])
        gain, term = vec_ref[2:3, :], vec_ref[3:4, :]
        final = normal * gain
        logit = jnp.sum(final * term, axis=-1, keepdims=True)
        live = (iota((seq, 1), 0) < place[1]).astype(F32)
        rest = jnp.exp(-jnp.abs(logit))
        weights = (jnp.maximum(logit, 0.0) + jnp.log1p(rest)) * live
        weights_ref[...] = jnp.broadcast_to(weights, weights_ref.shape)
        sigmoid = jnp.where(logit >= 0, 1.0, rest) / (1.0 + rest)
        grad_logit = cot_ref[:, 0:1] * live * sigmoid
        grad_final = grad_logit * term
        sums_ref[0:1, :] = jnp.sum(grad_final * normal, axis=0, keepdims=True)
        sums_ref[1:2, :] = jnp.sum(grad_logit * final, axis=0, keepdims=True)
        sums_ref[2:8, :] = jnp.zeros((6, sums_ref.shape[1]), F32)
        grad_mixed = norm_back(grad_final, normal, scale, gain)
        mixed_ref[...] = grad_mixed
        outer_ref[...] = grad_mixed.astype(BF)


def forward(place, att, emb, out_w, vec, cot, in_rows, back_rows):
    seq, width = att.shape
    units = in_rows.shape[0]
    step = 768
    shapes = (
        jax.ShapeDtypeStruct((seq, width), BF),
        jax.ShapeDtypeStruct((seq, width), F32),
        jax.ShapeDtypeStruct((seq, 128), F32),
        jax.ShapeDtypeStruct((seq, units), BF),
        jax.ShapeDtypeStruct((seq, units), F32),
        jax.ShapeDtypeStruct((seq, width), F32),
        jax.ShapeDtypeStruct((seq, width), BF),
        jax.ShapeDtypeStruct((seq, 128), F32),
        jax.ShapeDtypeStruct((8, width), F32),
    )
    return pl.pallas_call(
        forward_kernel,
        grid_spec=pltpu.PrefetchScalarGridSpec(
            num_scalar_prefetch=1,
            grid=(units // step,),
            in_specs=[
                whole((seq, width)),
                whole((seq, width)),
                whole((width, width)),
                whole(vec.shape),
                whole(cot.shape),
                pl.BlockSpec((step, width), lambda i, s: (i, 0)),
                pl.BlockSpec((step, width), lambda i, s: (i, 0)),
            ],
            out_specs=[
                whole((seq, width)),
                whole((seq, width)),
                whole((seq, 128)),
                pl.BlockSpec((seq, step), lambda i, s: (0, i)),
                pl.BlockSpec((seq, step), lambda i, s: (0, i)),
                whole((seq, width)),
                whole((seq, width)),
                whole((seq, 128)),
                whole((8, width)),
            ],
        ),
        out_shape=shapes,
        compiler_params=params(),
        name="forward",
    )(place, att, emb, out_w, vec, cot, in_rows, back_rows)


def backward_kernel(
    outer_ref, mixed_ref, normal_ref, scale_ref, out_w_ref, vec_ref, slope_ref, in_ref, back_ref,
    inner_ref, total_ref, branch_ref, att_ref, sums_ref,
):
    step = pl.program_id(0)
    grad_inner = (dot_nt(outer_ref[...], back_ref[...]) * slope_ref[...]).astype(BF)
    inner_ref[...] = grad_inner
    more = dot_nn(grad_inner, in_ref[...])

    @pl.when(step == 0)
    def _():
        total_ref[...] = mixed_ref[...] + more

    @pl.when(step > 0)
    def _():
        total_ref[...] += more

    @pl.when(step == pl.num_programs(0) - 1)
    def _():
        grad = total_ref[...]
        normal = normal_ref[...]
        sums_ref[0:1, :] = jnp.sum(grad * normal, axis=0, keepdims=True)
        sums_ref[1:2, :] = jnp.sum(grad, axis=0, keepdims=True)
        sums_ref[2:8, :] = jnp.zeros((6, sums_ref.shape[1]), F32)
        grad_sum = norm_back(grad, normal, scale_ref[:, 0:1], vec_ref[0:1, :])
        total_ref[...] = grad_sum
        branch = grad_sum.astype(BF)
        branch_ref[...] = branch
        att_ref[...] = dot_nt(branch, out_w_ref[...]).astype(BF)


def backward(outer, mixed, normal, scale, out_w, vec, slope, in_rows, back_rows):
    seq, width = outer.shape
    units = in_rows.shape[0]
    step = 768
    shapes = (
        jax.ShapeDtypeStruct((seq, units), BF),
        jax.ShapeDtypeStruct((seq, width), F32),
        jax.ShapeDtypeStruct((seq, width), BF),
        jax.ShapeDtypeStruct((seq, width), BF),
        jax.ShapeDtypeStruct((8, width), F32),
    )
    return pl.pallas_call(
        backward_kernel,
        grid=(units // step,),
        in_specs=[
            whole((seq, width)),
            whole((seq, width)),
            whole((seq, width)),
            whole((seq, 128)),
            whole((width, width)),
            whole(vec.shape),
            pl.BlockSpec((seq, step), lambda i: (0, i)),
            pl.BlockSpec((step, width), lambda i: (i, 0)),
            pl.BlockSpec((step, width), lambda i: (i, 0)),
        ],
        out_specs=[
            pl.BlockSpec((seq, step), lambda i: (0, i)),
            whole((seq, width)),
            whole((seq, width)),
            whole((seq, width)),
            whole((8, width)),
        ],
        out_shape=shapes,
        compiler_params=params(),
        name="backward",
    )(outer, mixed, normal, scale, out_w, vec, slope, in_rows, back_rows)


def unit_grad_kernel(keep_in, send_in, other_ref, keep_ref, send_ref):
    for source, out in ((send_in, send_ref), (keep_in, keep_ref)):
        out[...] = dot_tn(source[...], other_ref[...]).astype(BF).reshape(out.shape)


def unit_grad(rows, other, swap):
    seq, units = rows.shape
    width = other.shape[1]
    step = units // 4
    if swap:
        spec = pl.BlockSpec((2, 1, step // 2, width), lambda i: (0, i, 0, 0))
        shape = jax.ShapeDtypeStruct((2, 2, step // 2, width), BF)
    else:
        spec = pl.BlockSpec((1, 2, step // 2, width), lambda i: (i, 0, 0, 0))
        shape = jax.ShapeDtypeStruct((2, 2, step // 2, width), BF)
    keep, send = pl.pallas_call(
        unit_grad_kernel,
        grid=(2,),
        in_specs=[
            pl.BlockSpec((seq, step), lambda i: (0, i)),
            pl.BlockSpec((seq, step), lambda i: (0, 2 + i)),
            whole((seq, width)),
        ],
        out_specs=[spec, spec],
        out_shape=[shape, shape],
        compiler_params=params(),
        name="unit_grad",
    )(rows, rows, other)
    return keep.reshape(units // 2, width), send.reshape(units // 2, width)


def out_grad_kernel(order_ref, branch_ref, att_ref, first_ref, second_ref, keep_ref, send_ref):
    width = att_ref.shape[1]
    half = keep_ref.shape[0]
    hot = (iota((width, width), 0) == order_ref[0:1, :]).astype(F32).astype(BF)
    moved = dot_nn(branch_ref[...], hot).astype(BF)
    grad = dot_tn(moved, att_ref[...]).astype(BF)
    lines = jnp.concatenate([first_ref[...], second_ref[...], jnp.zeros((112, width), F32)], axis=0).astype(BF)
    sums = jnp.transpose(dot_nn(lines, hot)).astype(BF)
    keep_ref[:, :width] = grad[:half]
    send_ref[:, :width] = grad[half:]
    keep_ref[:, width:] = sums[:half]
    send_ref[:, width:] = sums[half:]


def out_grad(order, branch, att, first, second):
    width = att.shape[1]
    shape = jax.ShapeDtypeStruct((width // 2, width + 128), BF)
    args = (order, branch, att, first, second)
    return pl.pallas_call(
        out_grad_kernel,
        grid=(1,),
        in_specs=[whole(a.shape) for a in args],
        out_specs=[whole(shape.shape)] * 2,
        out_shape=[shape] * 2,
        compiler_params=params(),
        name="out_grad",
    )(*args)


def proj_grad_kernel(place, order_ref, emb_ref, keep_in, send_in, keep_ref, send_ref, moved_s):
    width = emb_ref.shape[1]

    @pl.when(pl.program_id(0) == 0)
    def _():
        hot = (iota((width, width), 0) == order_ref[0:1, :]).astype(F32).astype(BF)
        moved_s[...] = dot_nn(emb_ref[...], hot).astype(BF)

    for source, out in ((send_in, send_ref), (keep_in, keep_ref)):
        out[...] = dot_tn(moved_s[...], source[0]).astype(BF)


def proj_grad(place, order, emb, gproj):
    seq, width = emb.shape
    half = width // 2
    shape = jax.ShapeDtypeStruct((width, 3 * half), BF)
    return pl.pallas_call(
        proj_grad_kernel,
        grid_spec=pltpu.PrefetchScalarGridSpec(
            num_scalar_prefetch=1,
            grid=(3,),
            in_specs=[
                whole(order.shape),
                whole(emb.shape),
                pl.BlockSpec((1, seq, half), lambda i, s: (i, 0, s[0])),
                pl.BlockSpec((1, seq, half), lambda i, s: (i, 0, 1 - s[0])),
            ],
            out_specs=[pl.BlockSpec((width, half), lambda i, s: (0, i))] * 2,
            scratch_shapes=[pltpu.VMEM((seq, width), BF)],
        ),
        out_shape=[shape] * 2,
        compiler_params=params(),
        name="proj_grad",
    )(place, order, emb, gproj, gproj)


def swap_head(x):
    return lax.ppermute(x, "head", [(0, 1), (1, 0)])


def swap_dp(x, bit):
    return lax.ppermute(x, "dp", [(i, i ^ bit) for i in range(lax.axis_size("dp"))])


def scatter_sum(keep, recv, bits):
    for bit in bits:
        half = keep.shape[0] // 2
        out = keep[half:] + recv[half:]
        keep = keep[:half] + recv[:half]
        recv = swap_dp(out, bit)
    return keep.astype(F32) + recv.astype(F32)


def reversed_bits(count):
    bits = count.bit_length() - 1
    return [sum(((i >> b) & 1) << (bits - 1 - b) for b in range(bits)) for i in range(count)]


def swap_low(i):
    return (i & ~3) | ((i & 1) << 1) | ((i >> 1) & 1)


def body(
    token_ids,
    lengths,
    embed_table,
    qkv_weight,
    out_weight,
    first_gain,
    first_bias,
    in_weight,
    back_weight,
    second_gain,
    term_vector,
    cotangent,
):
    dp = lax.axis_index("dp")
    head = lax.axis_index("head")
    owners = lax.axis_size("dp")
    bits = [1 << b for b in range(owners.bit_length() - 1)]
    other_bits = [2, 1] + bits[2:]
    device = dp * 2 + head
    seq = token_ids.shape[0]
    table_rows, half = embed_table.shape
    width = 2 * half
    units = back_weight.shape[0]
    cap = 4 * seq // owners
    slots = owners * cap

    ids = token_ids.reshape(1, seq)
    ids = jnp.concatenate([ids, swap_head(ids)], axis=1)
    for bit in bits:
        ids = jnp.concatenate([ids, swap_dp(ids, bit)], axis=0)
    picked, asked, slot_row, slot_col = pick(dp.reshape(1), ids, embed_table, cap)
    got = lax.all_to_all(picked.reshape(owners, cap, half), "dp", split_axis=0, concat_axis=0, tiled=True)

    unit_order = device ^ jnp.array(reversed_bits(2 * owners), jnp.int32)
    back_rows = jnp.take(back_weight.reshape(2 * owners, -1, width), unit_order, axis=0).reshape(units, width)
    in_rows = jnp.take(in_weight.T.reshape(2 * owners, -1, width), unit_order, axis=0).reshape(units, width)
    other_weight = swap_head(qkv_weight)
    weight = jnp.where(
        head == 0,
        jnp.concatenate([qkv_weight, other_weight], axis=2),
        jnp.concatenate([other_weight, qkv_weight], axis=2),
    )
    out_block = width // (2 * owners)
    out_order = (unit_order[:, None] * out_block + jnp.arange(out_block, dtype=jnp.int32)[None, :]).reshape(1, width)
    row_block = width // owners // 2
    rev = reversed_bits(owners)
    first_half = (dp ^ jnp.array(rev, jnp.int32))[:, None] * (2 * row_block) + jnp.arange(row_block, dtype=jnp.int32)
    second_half = (dp ^ jnp.array([swap_low(r) for r in rev], jnp.int32))[:, None] * (2 * row_block) + (
        row_block + jnp.arange(row_block, dtype=jnp.int32)
    )
    proj_order = jnp.concatenate([first_half.reshape(1, half), second_half.reshape(1, half)], axis=1)
    vec = jnp.concatenate(
        [jnp.stack([first_gain, first_bias, second_gain, term_vector]), jnp.zeros((4, width), F32)], axis=0
    )
    cot = jnp.broadcast_to(cotangent.reshape(seq, 1), (seq, 128))
    place = jnp.stack([head, lengths[0]]).astype(jnp.int32)

    own, send = regather(slot_col, got.reshape(slots, half))
    other = swap_head(send)
    emb, proj, att, stat = attend(place, own, other, weight)
    low, normal, scale, active, slope, mixed, outer, weights, sums_two = forward(
        place, att, emb, out_weight, vec, cot, in_rows, back_rows
    )
    back_keep, back_send = unit_grad(active, outer, True)
    back_recv = swap_head(back_send)
    grad_inner, grad_sum, branch, grad_att, sums_one = backward(
        outer, mixed, normal, scale, out_weight, vec, slope, in_rows, back_rows
    )
    in_keep, in_send = unit_grad(grad_inner, low, False)
    in_recv = swap_head(in_send)
    grad_back = scatter_sum(back_keep, back_recv, other_bits)
    grad_in = scatter_sum(in_keep, in_recv, bits)
    gproj, grad_own, grad_send = attend_back(place, proj, grad_att, stat, weight, grad_sum)
    grad_other = swap_head(grad_send)
    sent = spread(slot_row, grad_own, grad_other, slots)
    arrived = lax.all_to_all(sent.reshape(owners, cap, half), "dp", split_axis=0, concat_axis=0, tiled=True)
    out_keep, out_send = out_grad(out_order, branch, att, sums_one, sums_two)
    grad_out = scatter_sum(out_keep, swap_head(out_send), bits)
    proj_keep, proj_send = proj_grad(place, proj_order, emb, gproj)
    proj_recv = swap_head(proj_send)
    grad_first = scatter_sum(proj_keep[:half], proj_recv[:half], bits)
    grad_second = scatter_sum(proj_keep[half:], proj_recv[half:], other_bits)
    grad_table = table_grad(asked.reshape(slots // 512, 512), arrived.reshape(slots, half), table_rows)
    grad_qkv = jnp.concatenate([grad_first, grad_second], axis=0)
    grad_qkv = grad_qkv.reshape(-1, 3, half).transpose(1, 0, 2)
    vectors = grad_out[:, width:]
    return (
        weights[:, 0],
        grad_table,
        grad_qkv,
        grad_out[:, :width].T,
        grad_in.T,
        grad_back,
        vectors[:, 0],
        vectors[:, 1],
        vectors[:, 8],
        vectors[:, 9],
    )


def solution(mesh):
    in_specs = (
        P(("dp", "head")),
        P(("dp", "head")),
        P("dp", "head"),
        P(None, None, "head"),
        P(),
        P(),
        P(),
        P(),
        P(),
        P(),
        P(),
        P(("dp", "head")),
    )
    out_specs = (
        P(("dp", "head")),
        P("dp", "head"),
        P(None, "dp", "head"),
        P(None, ("dp", "head")),
        P(None, ("dp", "head")),
        P(("dp", "head"), None),
        P(("dp", "head")),
        P(("dp", "head")),
        P(("dp", "head")),
        P(("dp", "head")),
    )
    return jax.shard_map(body, mesh=mesh, in_specs=in_specs, out_specs=out_specs, check_vma=False)
```

time: 864 us -> 324 us (0.38)
  waiting for transfers between devices: 495 us -> 100 us
  matrix products: 109 us -> 0 us
  Pallas kernels: 0 us -> 109 us
  blocking collectives: 101 us -> 0 us
  local copies, waits for them, and re-layouts: 75 us -> 32.3 us
  starting transfers between devices: 11.2 us -> 49.6 us
  other arithmetic: 49.6 us -> 30 us
  between operations: 16.4 us -> 1.77 us
    reduce_scatter x3 -> x0, waiting for transfers between devices: 366 us -> none  [the longest x1 142 us: body(): lax.psum_scatter(part_back, ('dp', 'head'), scatter_dimension=0, tiled=True)]
    pallas_call x0 -> x12, Pallas kernels: none -> 109 us  [the longest x1 19 us: attend_back(): pl.pallas_call(attend_back_kernel, grid_spec=pltpu.PrefetchScalarGridSpec...]
    dot_general x19 -> x0, matrix products: 98.3 us -> none  [the longest x1 20 us: body(): jnp.dot(normed_low, in_weight, preferred_element_type=jnp.float32)]
    ppermute x0 -> x32, waiting for transfers between devices: none -> 95.9 us  [the longest x24 94.8 us: swap_dp(): lax.ppermute(x, 'dp', [(i, i ^ bit) for i in range(lax.axis_size('dp'))])]
    unnamed x8 -> x0, waiting for transfers between devices: 88 us -> none
    unnamed x2 -> x0, blocking collectives: 73.4 us -> none
    ppermute x0 -> x32, starting transfers between devices: none -> 38.3 us  [the longest x24 36.4 us: swap_dp(): lax.ppermute(x, 'dp', [(i, i ^ bit) for i in range(lax.axis_size('dp'))])]
    all_to_all x2, waiting for transfers between devices: 33.6 us -> 4.25 us  [the longest x1 4.25 us: body(): lax.all_to_all(picked.reshape(owners, cap, half), 'dp', split_axis=0, con...]
  transfers between devices with their start and end apart: 8 -> 34, of which waited for: 6 -> 20; matrix products, arithmetic and copies ran while one was open for 9% -> 15% of each run, Pallas kernels for 0% -> 15%
where the time goes in v1:
time: 324 us; the launch traced here: 323 us
  Pallas kernels  109 us (34%)
  waiting for transfers between devices  100 us (31%)
  starting transfers between devices  49.6 us (15%)
  local copies, waits for them, and re-layouts  32.3 us (10%)
  other arithmetic  30 us (9%)
    ppermute x24, waiting for transfers between devices, swap_dp(): lax.ppermute(x, 'dp', [(i, i ^ bit) for i in range(lax.axis_size('dp'))])  94.8 us
    ppermute x24, starting transfers between devices, swap_dp(): lax.ppermute(x, 'dp', [(i, i ^ bit) for i in range(lax.axis_size('dp'))])  36.4 us
    pallas_call x1, Pallas kernels, attend_back(): pl.pallas_call(attend_back_kernel, grid_spec=pltpu.PrefetchScalarGridSpec...  19 us
    pallas_call x1, Pallas kernels, forward(): pl.pallas_call(forward_kernel, grid_spec=pltpu.PrefetchScalarGridSpec(num...  17.4 us
    unnamed x60, local copies, waits for them, and re-layouts  15.9 us
    pallas_call x1, Pallas kernels, pick(): pl.pallas_call(pick_kernel, grid_spec=pltpu.PrefetchScalarGridSpec(num_sc...  13.9 us
    pallas_call x1, Pallas kernels, backward(): pl.pallas_call(backward_kernel, grid=(units // step,), in_specs=[whole((s...  13.5 us
    pallas_call x1, Pallas kernels, attend(): pl.pallas_call(attend_kernel, grid_spec=pltpu.PrefetchScalarGridSpec(num_...  13.4 us
  transfers between devices with their start and end apart: 34, of which 20 were waited for; matrix products, arithmetic and copies ran while one was open for 15% of the time, Pallas kernels for 15%

profile of v1, /device:TPU:0, one launch (start us, length us, event | category | flops | bytes accessed | tf_op | source)
XLA Modules:
  0.0 322.6 jit_solution(13992199391195287732)
XLA Ops:
  23.4 13.9 %pick.1 = (bf16[2048,384]{1,0:T(8,128)(2,1)}, f32[16,128]{1,0:T(8,128)S(1)}, f32[8,1024]{1,0:T(8,128)S(1)}, f32[1024,128]{1,0:T(8,128)S(1)}) custom-call(s32[1]{0:T(128)} %bitcast.1.place, s32[16,1024]{1,0:T(8,128)S(1)} %concatenate.37.ids_ref, bf16[1920,384]{1,0:T(8,128)(2,1)S(1)} %copy-done.3), custom_call_target="tpu_custom_call" | custom-call | tf_op jit(solution)/shard_map/pick/pallas_call | solution.py:102
  37.3 7.4 %all-to-all-start = ((bf16[16,128,384]{2,1,0:T(8,128)(2,1)}), bf16[16,128,384]{2,1,0:T(8,128)(2,1)S(1)}, u32[]{:S(2)}, u32[]{:S(2)}) async-start(bf16[16,128,384]{2,1,0:T(8,128)(2,1)} %bitcast.3), calls=%async_computation | async-start | bytes 3145728 | tf_op jit(solution)/shard_map/all_to_all | solution.py:692
  45.5 6.6 %copy.26 = bf16[768,3072]{0,1:T(8,128)(2,1)} copy(bf16[768,3072]{1,0:T(8,128)(2,1)} %param.24) | data formatting | bytes 9437184 | tf_op args[7]
  52.2 5.3 %gather_fusion = bf16[32,96,768]{2,1,0:T(8,128)(2,1)} fusion(bf16[32,96,768]{2,1,0:T(8,128)(2,1)} %bitcast.34, s32[1024]{0:T(1024)S(1)} %pad_clamp_fusion), kind=kCustom, calls=%fused_computation.clone | custom fusion | bytes 9437312 | tf_op jit(solution)/shard_map/jit(_take)/gather | solution.py:696
  57.5 5.3 %gather_fusion.1 = bf16[32,96,768]{2,1,0:T(8,128)(2,1)} fusion(bf16[32,96,768]{2,1,0:T(8,128)(2,1)} %bitcast.35, s32[1024]{0:T(1024)S(1)} %pad_clamp_fusion), kind=kCustom, calls=%fused_computation.1.clone | custom fusion | bytes 9437312 | tf_op jit(solution)/shard_map/jit(_take)/gather | solution.py:695
  62.9 8.3 %broadcast_select_fusion = (bf16[32,96,768]{2,1,0:T(8,128)(2,1)}, bf16[32,96,768]{2,1,0:T(8,128)(2,1)}) fusion(bf16[32,96,768]{2,1,0:T(8,128)(2,1)} %gather_fusion.1, pred[32]{0:T(512)(128)(4,1)S(1)} %get-tuple-element.95, bf16[32,96,768]{2,1,0:T(8,128)(2,1)} %gather_fusion), kind=kLoop, calls=%fused_computation.2 | loop fusion | flops 4718592 | bytes 18874400 | tf_op jit(solution)/shard_map/jit(_take)/select_n | solution.py:695
  71.2 4.2 %all-to-all-done = bf16[16,128,384]{2,1,0:T(8,128)(2,1)S(1)} async-done(((bf16[16,128,384]{2,1,0:T(8,128)(2,1)}), bf16[16,128,384]{2,1,0:T(8,128)(2,1)S(1)}, u32[]{:S(2)}, u32[]{:S(2)}) %all-to-all-start) | async-done | bytes 1572896 | tf_op jit(solution)/shard_map/all_to_all | solution.py:692
  78.2 4.8 %maximum_select_fusion.weight_ref = bf16[3,768,768]{2,1,0:T(8,128)(2,1)} fusion(bf16[3,768,384]{2,1,0:T(8,128)(2,1)} %collective-permute-done.6, bf16[3,768,384]{2,1,0:T(8,128)(2,1)} %param.20, pred[]{:T(512)S(6)} %eq.3), kind=kLoop, calls=%fused_computation.4 | loop fusion | flops 15925248 | bytes 7077889 | tf_op jit(solution)/shard_map/jit(_where)/select_n | solution.py:698
  83.0 13.4 %attend.1 = (bf16[512,768]{1,0:T(8,128)(2,1)S(1)}, bf16[3,512,768]{2,1,0:T(8,128)(2,1)S(1)}, bf16[512,768]{1,0:T(8,128)(2,1)S(1)}, f32[6,8,512]{2,1,0:T(8,128)S(1)}) custom-call(s32[2]{0:T(128)S(1)} %pad_add_fusion.5.place, bf16[512,384]{1,0:T(8,128)(2,1)S(1)} %get-tuple-element.48.own_ref, bf16[512,384]{1,0:T(8,128)(2,1)S(1)} %collective-permute-done.5.other_ref, ...), custom_call_target="tpu_custom_call" | custom-call | tf_op jit(solution)/shard_map/attend/pallas_call | solution.py:243
  98.0 17.4 %forward.1 = (bf16[512,768]{1,0:T(8,128)(2,1)S(1)}, f32[512,768]{1,0:T(8,128)}, f32[512,128]{1,0:T(8,128)S(1)}, bf16[512,3072]{1,0:T(8,128)(2,1)}, f32[512,3072]...) custom-call(s32[2]{0:T(128)S(1)} %pad_add_fusion.5.place, ...), custom_call_target="tpu_custom_call" | custom-call | tf_op jit(solution)/shard_map/forward/pallas_call | solution.py:437
  117.0 13.5 %backward.1 = (bf16[512,3072]{1,0:T(8,128)(2,1)}, f32[512,768]{1,0:T(8,128)S(1)}, bf16[512,768]{1,0:T(8,128)(2,1)S(1)}, bf16[512,768]{1,0:T(8,128)(2,1)S(1)}, f32[8,768]{1,0:T(8,128)S(1)}) custom-call(bf16[512,768]{1,0:T(8,128)(2,1)S(1)} %get-tuple-element.56.outer_ref.other_ref, f32[512,768]{1,0:T(8,128)} %get-tuple-element.57.mixed_ref, ...), custom_call_target="tpu_custom_call" | custom-call | tf_op jit(solution)/shard_map/backward/pallas_call | solution.py:511
  136.1 19.0 %attend_back.1 = (bf16[3,512,768]{2,1,0:T(8,128)(2,1)S(1)}, bf16[512,384]{1,0:T(8,128)(2,1)S(1)}, bf16[512,384]{1,0:T(8,128)(2,1)S(1)}) custom-call(s32[2]{0:T(128)S(1)} %pad_add_fusion.5.place, bf16[3,512,768]{2,1,0:T(8,128)(2,1)} %copy-done.2, bf16[512,768]{1,0:T(8,128)(2,1)S(1)} %copy-done.7, f32[6,8,512]{2,1,0:T(8,128)S(1)} %get-tuple-element.62.stat_ref, ...), custom_call_target="tpu_custom_call" | custom-call | tf_op jit(solution)/shard_map/attend_back/pallas_call | solution.py:330
  156.5 6.8 %proj_grad.1 = (bf16[768,1152]{1,0:T(8,128)(2,1)S(1)}, bf16[768,1152]{1,0:T(8,128)(2,1)}) custom-call(s32[2]{0:T(128)S(1)} %pad_add_fusion.5.place, s32[1,768]{1,0:T(1,128)S(1)} %pad_add_fusion.4.order_ref, bf16[512,768]{1,0:T(8,128)(2,1)S(1)} %get-tuple-element.51.emb_ref, bf16[3,512,768]{2,1,0:T(8,128)(2,1)} %copy-done, bf16[3,512,768]{2,1,0:T(8,128)(2,1)} %copy-done), custom_call_target="tpu_custom_call" | custom-call | tf_op jit(solution)/shard_map/proj_grad/pallas_call | solution.py:614
  166.0 5.5 %unit_grad.3 = (bf16[2,2,384,768]{3,2,1,0:T(8,128)(2,1)S(1)}, bf16[2,2,384,768]{3,2,1,0:T(8,128)(2,1)}) custom-call(bf16[512,3072]{1,0:T(8,128)(2,1)} %get-tuple-element.78.keep_in.send_in, bf16[512,3072]{1,0:T(8,128)(2,1)} %get-tuple-element.78.keep_in.send_in, bf16[512,768]{1,0:T(8,128)(2,1)S(1)} %get-tuple-element.56.outer_ref.other_ref), custom_call_target="tpu_custom_call" | custom-call | tf_op jit(solution)/shard_map/unit_grad/pallas_call | solution.py:553
  171.7 4.9 %unit_grad.2 = (bf16[2,2,384,768]{3,2,1,0:T(8,128)(2,1)S(1)}, bf16[2,2,384,768]{3,2,1,0:T(8,128)(2,1)}) custom-call(bf16[512,3072]{1,0:T(8,128)(2,1)} %get-tuple-element.74.keep_in.send_in, bf16[512,3072]{1,0:T(8,128)(2,1)} %get-tuple-element.74.keep_in.send_in, bf16[512,768]{1,0:T(8,128)(2,1)S(1)} %copy-done.5), custom_call_target="tpu_custom_call" | custom-call | tf_op jit(solution)/shard_map/unit_grad/pallas_call | solution.py:553
  196.4 3.8 %all-to-all-start.1 = ((bf16[16,128,384]{2,1,0:T(8,128)(2,1)}), bf16[16,128,384]{2,1,0:T(8,128)(2,1)S(1)}, u32[]{:S(2)}, u32[]{:S(2)}) async-start(bf16[16,128,384]{2,1,0:T(8,128)(2,1)} %bitcast.10), calls=%async_computation.1 | async-start | bytes 3145728 | tf_op jit(solution)/shard_map/all_to_all | solution.py:736
  206.3 32.2 %collective-permute-done.21 = bf16[24,896]{1,0:T(8,128)(2,1)S(1)} collective-permute-done((bf16[24,896]{1,0:T(8,128)(2,1)S(1)}, bf16[24,896]{1,0:T(8,128)(2,1)S(1)}, u32[]{:S(2)}, u32[]{:S(2)}) %collective-permute-start.21) | collective-permute-done | bytes 43040 | tf_op jit(solution)/shard_map/ppermute | solution.py:639
  242.6 10.9 %collective-permute-done.13 = bf16[192,1152]{1,0:T(8,128)(2,1)S(1)} collective-permute-done((bf16[192,1152]{1,0:T(8,128)(2,1)S(1)}, bf16[192,1152]{1,0:T(8,128)(2,1)S(1)}, u32[]{:S(2)}, u32[]{:S(2)}) %collective-permute-start.13) | collective-permute-done | bytes 442400 | tf_op jit(solution)/shard_map/ppermute | solution.py:639
  272.4 9.1 %collective-permute-done.28 = bf16[768,768]{1,0:T(8,128)(2,1)S(1)} collective-permute-done((bf16[768,768]{1,0:T(8,128)(2,1)S(1)}, bf16[768,768]{1,0:T(8,128)(2,1)S(1)}, u32[]{:S(2)}, u32[]{:S(2)}) %collective-permute-start.28) | collective-permute-done | bytes 1179680 | tf_op jit(solution)/shard_map/ppermute | solution.py:639
  283.1 6.3 %collective-permute-done.23 = bf16[768,768]{1,0:T(8,128)(2,1)S(1)} collective-permute-done((bf16[768,768]{1,0:T(8,128)(2,1)S(1)}, bf16[768,768]{1,0:T(8,128)(2,1)S(1)}, u32[]{:S(2)}, u32[]{:S(2)}) %collective-permute-start.23) | collective-permute-done | bytes 1179680 | tf_op jit(solution)/shard_map/ppermute | solution.py:639
  290.5 7.0 %collective-permute-done.29 = bf16[384,768]{1,0:T(8,128)(2,1)S(1)} collective-permute-done((bf16[384,768]{1,0:T(8,128)(2,1)S(1)}, bf16[384,768]{1,0:T(8,128)(2,1)S(1)}, u32[]{:S(2)}, u32[]{:S(2)}) %collective-permute-start.29) | collective-permute-done | bytes 589856 | tf_op jit(solution)/shard_map/ppermute | solution.py:639
  301.2 5.5 %table_grad.1 = f32[1920,384]{1,0:T(8,128)} custom-call(f32[4,512]{1,0:T(4,128)S(1)} %reshape.162.asked_ref, bf16[2048,384]{1,0:T(8,128)(2,1)S(1)} %bitcast.28), custom_call_target="tpu_custom_call" | custom-call | tf_op jit(solution)/shard_map/table_grad/pallas_call | solution.py:178
  307.7 5.4 %collective-permute-done.25 = bf16[192,768]{1,0:T(8,128)(2,1)} collective-permute-done((bf16[192,768]{1,0:T(8,128)(2,1)S(1)}, bf16[192,768]{1,0:T(8,128)(2,1)}, u32[]{:S(2)}, u32[]{:S(2)}) %collective-permute-start.25) | collective-permute-done | bytes 294944 | tf_op jit(solution)/shard_map/ppermute | solution.py:639
  315.5 5.4 %collective-permute-done.26 = bf16[96,768]{1,0:T(8,128)(2,1)S(1)} collective-permute-done((bf16[96,768]{1,0:T(8,128)(2,1)S(1)}, bf16[96,768]{1,0:T(8,128)(2,1)S(1)}, u32[]{:S(2)}, u32[]{:S(2)}) %collective-permute-start.26) | collective-permute-done | bytes 147488 | tf_op jit(solution)/shard_map/ppermute | solution.py:639
  (177 shorter events, 98.7 us)
Async XLA Ops:
  37.3 38.1 %all-to-all-start = ((bf16[16,128,384]{2,1,0:T(8,128)(2,1)}), bf16[16,128,384]{2,1,0:T(8,128)(2,1)S(1)}, u32[]{:S(2)}, u32[]{:S(2)}) async-start(bf16[16,128,384]{2,1,0:T(8,128)(2,1)} %bitcast.3), calls=%async_computation | async-start | bytes 3145728 | tf_op jit(solution)/shard_map/all_to_all | solution.py:692
  44.8 33.4 %collective-permute-start.6 = (bf16[3,768,384]{2,1,0:T(8,128)(2,1)}, bf16[3,768,384]{2,1,0:T(8,128)(2,1)}, u32[]{:S(2)}, u32[]{:S(2)}) collective-permute-start(bf16[3,768,384]{2,1,0:T(8,128)(2,1)} %param.20), channel_id=1, source_target_pairs={{0,1},{1,0},{2,3},{3,2},{4,5},{5,4},{6,7},{7,6},{8,9},{9,8},{10,11... | collective-permute-start | bytes 5308424 | tf_op jit(solution)/shard_map/ppermute | solution.py:635
  134.1 29.3 %collective-permute-start.17 = (bf16[384,896]{1,0:T(8,128)(2,1)}, bf16[384,896]{1,0:T(8,128)(2,1)}, u32[]{:S(2)}, u32[]{:S(2)}) collective-permute-start(bf16[384,896]{1,0:T(8,128)(2,1)} %get-tuple-element.73), channel_id=1, source_target_pairs={{0,1},{1,0},{2,3},{3,2},{4,5},{5,4},{6,7},{7,6},{8,9},{9,8},{10,11... | collective-permute-start | bytes 2064392 | tf_op jit(solution)/shard_map/ppermute | solution.py:635
  163.4 39.8 %collective-permute-start.8 = (bf16[768,1152]{1,0:T(8,128)(2,1)}, bf16[768,1152]{1,0:T(8,128)(2,1)}, u32[]{:S(2)}, u32[]{:S(2)}) collective-permute-start(bf16[768,1152]{1,0:T(8,128)(2,1)} %get-tuple-element.68), channel_id=1, source_target_pairs={{0,1},{1,0},{2,3},{3,2},{4,5},{5,4},{6,7},{7,6},{8,9},{9,8},{10,11... | collective-permute-start | bytes 5308424 | tf_op jit(solution)/shard_map/ppermute | solution.py:635
  165.4 13.2 %collective-permute-start.18 = (bf16[192,896]{1,0:T(8,128)(2,1)}, bf16[192,896]{1,0:T(8,128)(2,1)S(1)}, u32[]{:S(2)}, u32[]{:S(2)}) collective-permute-start(bf16[192,896]{1,0:T(8,128)(2,1)} %get-tuple-element.114), channel_id=1, source_target_pairs={{0,2},{2,0},{4,6},{6,4},{8,10},{10,8},{12,14},{14,12},{16,18},{18,... | collective-permute-start | bytes 1032200 | tf_op jit(solution)/shard_map/ppermute | solution.py:639
  171.5 83.6 %collective-permute-start.27 = (bf16[1536,768]{1,0:T(8,128)(2,1)}, bf16[1536,768]{1,0:T(8,128)(2,1)}, u32[]{:S(2)}, u32[]{:S(2)}) collective-permute-start(bf16[1536,768]{1,0:T(8,128)(2,1)} %bitcast.19), channel_id=1, source_target_pairs={{0,1},{1,0},{2,3},{3,2},{4,5},{5,4},{6,7},{7,6},{8,9},{9,8},{10,11... | collective-permute-start | bytes 7077896 | tf_op jit(solution)/shard_map/ppermute | solution.py:635
  176.6 82.6 %collective-permute-start.22 = (bf16[1536,768]{1,0:T(8,128)(2,1)}, bf16[1536,768]{1,0:T(8,128)(2,1)}, u32[]{:S(2)}, u32[]{:S(2)}) collective-permute-start(bf16[1536,768]{1,0:T(8,128)(2,1)} %bitcast.15), channel_id=1, source_target_pairs={{0,1},{1,0},{2,3},{3,2},{4,5},{5,4},{6,7},{7,6},{8,9},{9,8},{10,11... | collective-permute-start | bytes 7077896 | tf_op jit(solution)/shard_map/ppermute | solution.py:635
  176.9 15.9 %collective-permute-start.7 = (bf16[512,384]{1,0:T(8,128)(2,1)S(1)}, bf16[512,384]{1,0:T(8,128)(2,1)S(1)}, u32[]{:S(2)}, u32[]{:S(2)}) collective-permute-start(bf16[512,384]{1,0:T(8,128)(2,1)S(1)} %copy-done.15), channel_id=1, source_target_pairs={{0,1},{1,0},{2,3},{3,2},{4,5},{5,4},{6,7},{7,6},{8,9},{9,8},{10,11... | collective-permute-start | bytes 1179656 | tf_op jit(solution)/shard_map/ppermute | solution.py:635
  180.4 7.6 %collective-permute-start.19 = (bf16[96,896]{1,0:T(8,128)(2,1)S(1)}, bf16[96,896]{1,0:T(8,128)(2,1)S(1)}, u32[]{:S(2)}, u32[]{:S(2)}) collective-permute-start(bf16[96,896]{1,0:T(8,128)(2,1)S(1)} %get-tuple-element.124), channel_id=1, source_target_pairs={{0,4},{2,6},{4,0},{6,2},{8,12},{10,14},{12,8},{14,10},{16,20},{18,... | collective-permute-start | bytes 516104 | tf_op jit(solution)/shard_map/ppermute | solution.py:639
  188.6 11.6 %collective-permute-start.20 = (bf16[48,896]{1,0:T(8,128)(2,1)}, bf16[48,896]{1,0:T(8,128)(2,1)S(1)}, u32[]{:S(2)}, u32[]{:S(2)}) collective-permute-start(bf16[48,896]{1,0:T(8,128)(2,1)} %get-tuple-element.130), channel_id=1, source_target_pairs={{0,8},{2,10},{4,12},{6,14},{8,0},{10,2},{12,4},{14,6},{16,24},{18,... | collective-permute-start | bytes 258056 | tf_op jit(solution)/shard_map/ppermute | solution.py:639
  196.4 104.8 %all-to-all-start.1 = ((bf16[16,128,384]{2,1,0:T(8,128)(2,1)}), bf16[16,128,384]{2,1,0:T(8,128)(2,1)S(1)}, u32[]{:S(2)}, u32[]{:S(2)}) async-start(bf16[16,128,384]{2,1,0:T(8,128)(2,1)} %bitcast.10), calls=%async_computation.1 | async-start | bytes 3145728 | tf_op jit(solution)/shard_map/all_to_all | solution.py:736
  200.3 38.2 %collective-permute-start.21 = (bf16[24,896]{1,0:T(8,128)(2,1)S(1)}, bf16[24,896]{1,0:T(8,128)(2,1)S(1)}, u32[]{:S(2)}, u32[]{:S(2)}) collective-permute-start(bf16[24,896]{1,0:T(8,128)(2,1)S(1)} %slice_add_fusion.38), channel_id=1, source_target_pairs={{0,16},{2,18},{4,20},{6,22},{8,24},{10,26},{12,28},{14,30},{16,0},... | collective-permute-start | bytes 129032 | tf_op jit(solution)/shard_map/ppermute | solution.py:639
  204.8 37.6 %collective-permute-start.9 = (bf16[192,1152]{1,0:T(8,128)(2,1)S(1)}, bf16[192,1152]{1,0:T(8,128)(2,1)S(1)}, u32[]{:S(2)}, u32[]{:S(2)}) collective-permute-start(bf16[192,1152]{1,0:T(8,128)(2,1)S(1)} %get-tuple-element.100), channel_id=1, source_target_pairs={{0,2},{2,0},{4,6},{6,4},{8,10},{10,8},{12,14},{14,12},{16,18},{18,... | collective-permute-start | bytes 1327112 | tf_op jit(solution)/shard_map/ppermute | solution.py:639
  239.9 13.6 %collective-permute-start.13 = (bf16[192,1152]{1,0:T(8,128)(2,1)S(1)}, bf16[192,1152]{1,0:T(8,128)(2,1)S(1)}, u32[]{:S(2)}, u32[]{:S(2)}) collective-permute-start(bf16[192,1152]{1,0:T(8,128)(2,1)S(1)} %get-tuple-element.98), channel_id=1, source_target_pairs={{0,4},{2,6},{4,0},{6,2},{8,12},{10,14},{12,8},{14,10},{16,20},{18,... | collective-permute-start | bytes 1327112 | tf_op jit(solution)/shard_map/ppermute | solution.py:639
  242.5 19.3 %collective-permute-start.10 = (bf16[96,1152]{1,0:T(8,128)(2,1)S(1)}, bf16[96,1152]{1,0:T(8,128)(2,1)S(1)}, u32[]{:S(2)}, u32[]{:S(2)}) collective-permute-start(bf16[96,1152]{1,0:T(8,128)(2,1)S(1)} %get-tuple-element.120), channel_id=1, source_target_pairs={{0,4},{2,6},{4,0},{6,2},{8,12},{10,14},{12,8},{14,10},{16,20},{18,... | collective-permute-start | bytes 663560 | tf_op jit(solution)/shard_map/ppermute | solution.py:639
  253.6 8.3 %collective-permute-start.14 = (bf16[96,1152]{1,0:T(8,128)(2,1)S(1)}, bf16[96,1152]{1,0:T(8,128)(2,1)S(1)}, u32[]{:S(2)}, u32[]{:S(2)}) collective-permute-start(bf16[96,1152]{1,0:T(8,128)(2,1)S(1)} %get-tuple-element.122), channel_id=1, source_target_pairs={{0,2},{2,0},{4,6},{6,4},{8,10},{10,8},{12,14},{14,12},{16,18},{18,... | collective-permute-start | bytes 663560 | tf_op jit(solution)/shard_map/ppermute | solution.py:639
  257.1 24.4 %collective-permute-start.28 = (bf16[768,768]{1,0:T(8,128)(2,1)S(1)}, bf16[768,768]{1,0:T(8,128)(2,1)S(1)}, u32[]{:S(2)}, u32[]{:S(2)}) collective-permute-start(bf16[768,768]{1,0:T(8,128)(2,1)S(1)} %get-tuple-element.104), channel_id=1, source_target_pairs={{0,4},{2,6},{4,0},{6,2},{8,12},{10,14},{12,8},{14,10},{16,20},{18,... | collective-permute-start | bytes 3538952 | tf_op jit(solution)/shard_map/ppermute | solution.py:639
  261.0 28.3 %collective-permute-start.23 = (bf16[768,768]{1,0:T(8,128)(2,1)S(1)}, bf16[768,768]{1,0:T(8,128)(2,1)S(1)}, u32[]{:S(2)}, u32[]{:S(2)}) collective-permute-start(bf16[768,768]{1,0:T(8,128)(2,1)S(1)} %get-tuple-element.110), channel_id=1, source_target_pairs={{0,2},{2,0},{4,6},{6,4},{8,10},{10,8},{12,14},{14,12},{16,18},{18,... | collective-permute-start | bytes 3538952 | tf_op jit(solution)/shard_map/ppermute | solution.py:639
  268.2 22.2 %collective-permute-start.16 = (bf16[24,1152]{1,0:T(8,128)(2,1)S(1)}, bf16[24,1152]{1,0:T(8,128)(2,1)S(1)}, u32[]{:S(2)}, u32[]{:S(2)}) collective-permute-start(bf16[24,1152]{1,0:T(8,128)(2,1)S(1)} %slice_add_fusion.34), channel_id=1, source_target_pairs={{0,16},{2,18},{4,20},{6,22},{8,24},{10,26},{12,28},{14,30},{16,0},... | collective-permute-start | bytes 165896 | tf_op jit(solution)/shard_map/ppermute | solution.py:639
  281.6 15.9 %collective-permute-start.29 = (bf16[384,768]{1,0:T(8,128)(2,1)S(1)}, bf16[384,768]{1,0:T(8,128)(2,1)S(1)}, u32[]{:S(2)}, u32[]{:S(2)}) collective-permute-start(bf16[384,768]{1,0:T(8,128)(2,1)S(1)} %get-tuple-element.102), channel_id=1, source_target_pairs={{0,2},{2,0},{4,6},{6,4},{8,10},{10,8},{12,14},{14,12},{16,18},{18,... | collective-permute-start | bytes 1769480 | tf_op jit(solution)/shard_map/ppermute | solution.py:639
  289.5 9.9 %collective-permute-start.24 = (bf16[384,768]{1,0:T(8,128)(2,1)S(1)}, bf16[384,768]{1,0:T(8,128)(2,1)S(1)}, u32[]{:S(2)}, u32[]{:S(2)}) collective-permute-start(bf16[384,768]{1,0:T(8,128)(2,1)S(1)} %get-tuple-element.108), channel_id=1, source_target_pairs={{0,4},{2,6},{4,0},{6,2},{8,12},{10,14},{12,8},{14,10},{16,20},{18,... | collective-permute-start | bytes 1769480 | tf_op jit(solution)/shard_map/ppermute | solution.py:639
  298.3 8.6 %collective-permute-start.30 = (bf16[192,768]{1,0:T(8,128)(2,1)}, bf16[192,768]{1,0:T(8,128)(2,1)S(1)}, u32[]{:S(2)}, u32[]{:S(2)}) collective-permute-start(bf16[192,768]{1,0:T(8,128)(2,1)} %get-tuple-element.116), channel_id=1, source_target_pairs={{0,8},{2,10},{4,12},{6,14},{8,0},{10,2},{12,4},{14,6},{16,24},{18,... | collective-permute-start | bytes 884744 | tf_op jit(solution)/shard_map/ppermute | solution.py:639
  299.5 13.6 %collective-permute-start.25 = (bf16[192,768]{1,0:T(8,128)(2,1)S(1)}, bf16[192,768]{1,0:T(8,128)(2,1)}, u32[]{:S(2)}, u32[]{:S(2)}) collective-permute-start(bf16[192,768]{1,0:T(8,128)(2,1)S(1)} %get-tuple-element.118), channel_id=1, source_target_pairs={{0,8},{2,10},{4,12},{6,14},{8,0},{10,2},{12,4},{14,6},{16,24},{18,... | collective-permute-start | bytes 884744 | tf_op jit(solution)/shard_map/ppermute | solution.py:639
  306.9 7.8 %collective-permute-start.31 = (bf16[96,768]{1,0:T(8,128)(2,1)S(1)}, bf16[96,768]{1,0:T(8,128)(2,1)S(1)}, u32[]{:S(2)}, u32[]{:S(2)}) collective-permute-start(bf16[96,768]{1,0:T(8,128)(2,1)S(1)} %slice_add_fusion.24), channel_id=1, source_target_pairs={{0,16},{2,18},{4,20},{6,22},{8,24},{10,26},{12,28},{14,30},{16,0},... | collective-permute-start | bytes 442376 | tf_op jit(solution)/shard_map/ppermute | solution.py:639
  (39 other events, 325.1 us)

commit v2 on v1

v2 whole, which is shorter than its diff:
```python
import functools

import jax
import jax.numpy as jnp
from jax import lax
from jax.experimental import pallas as pl
from jax.experimental.pallas import tpu as pltpu
from jax.sharding import PartitionSpec as P

HDIM = 64
LOG2E = 1.4426950408889634
BF = jnp.bfloat16
F32 = jnp.float32
VMEM_LIMIT = 40 * 1024 * 1024


def dot_nn(a, b):
    return lax.dot_general(a, b, (((1,), (0,)), ((), ())), preferred_element_type=F32)


def dot_nt(a, b):
    return lax.dot_general(a, b, (((1,), (1,)), ((), ())), preferred_element_type=F32)


def dot_tn(a, b):
    return lax.dot_general(a, b, (((0,), (0,)), ((), ())), preferred_element_type=F32)


def iota(shape, dim):
    return lax.broadcasted_iota(jnp.int32, shape, dim)


def params(**more):
    return pltpu.CompilerParams(vmem_limit_bytes=VMEM_LIMIT, **more)


def whole(shape):
    return pl.BlockSpec(shape, lambda *_: (0,) * len(shape))


def cost(micros):
    return pl.CostEstimate(flops=0, bytes_accessed=int(micros * 1e3), transcendentals=0)


ANY = pl.BlockSpec(memory_space=pl.ANY)


def run(kernel, name, micros, scalars, args, grid, in_specs, out_specs, shapes, scratch=(), after=()):
    first, count = len(scalars) + len(args), len(after)

    def inner(*refs):
        kernel(*refs[:first], *refs[first + count :])

    return pl.pallas_call(
        inner,
        grid_spec=pltpu.PrefetchScalarGridSpec(
            num_scalar_prefetch=len(scalars),
            grid=grid,
            in_specs=list(in_specs) + [ANY] * count,
            out_specs=out_specs,
            scratch_shapes=list(scratch),
        ),
        out_shape=shapes,
        compiler_params=params(),
        cost_estimate=cost(micros),
        name=name,
    )(*scalars, *args, *after)


def pick_kernel(place, ids_ref, table_ref, picked_ref, asked_ref, row_ref, col_ref, rank_s, away_s, hot_s):
    owners, block = ids_ref.shape
    rows = table_ref.shape[0]
    cap = picked_ref.shape[0] // owners
    dp = place[0]
    ids = ids_ref[...]
    away = ids - dp * rows
    mine = (away >= 0) & (away < rows)
    floor = iota((owners, block), 0) * rows
    own_ids = ids_ref[0:1, :]
    marks = (own_ids >= floor) & (own_ids < floor + rows)
    both = jnp.concatenate([mine.astype(F32), marks.astype(F32)], axis=0).astype(BF)
    upto = (iota((block, block), 0) <= iota((block, block), 1)).astype(F32).astype(BF)
    counts = dot_nn(both, upto)
    rank_s[...] = (jnp.where(mine, counts[:owners], 0.0) - 1.0).astype(jnp.int32)
    away_s[...] = away
    spot = jnp.where(marks, counts[owners:] - 1.0 + iota((owners, block), 0).astype(F32) * cap, 0.0)
    slot = jnp.sum(spot, axis=0, keepdims=True)
    row_ref[...] = jnp.broadcast_to(slot, row_ref.shape)
    col_ref[...] = jnp.transpose(jnp.broadcast_to(slot, (128, block)))
    group = hot_s.shape[0] // cap
    spots = iota((cap, block), 0)
    lanes = iota((cap, 128), 1)

    def per_group(g, table_of):
        for i in range(group):
            j = g * group + i
            r = j ^ dp
            found = jnp.where(spots == rank_s[pl.ds(r, 1), :], away_s[pl.ds(r, 1), :], 0)
            asked = jnp.sum(found, axis=1, keepdims=True)
            table_of = jnp.where(lanes == j, asked, table_of)
            hot_s[i * cap : (i + 1) * cap, :] = (iota((cap, rows), 1) == asked).astype(F32).astype(BF)
        size = group * cap
        picked_ref[pl.ds(pl.multiple_of(g * size, size), size), :] = dot_nn(hot_s[...], table_ref[...]).astype(BF)
        return table_of

    table_of = lax.fori_loop(0, owners // group, per_group, jnp.zeros((cap, 128), jnp.int32))
    asked_ref[...] = jnp.transpose(table_of.astype(F32))


def pick(dp, ids, table, cap):
    owners, block = ids.shape
    rows, half = table.shape
    group = min(owners, max(1, 512 // cap))
    shapes = (
        jax.ShapeDtypeStruct((owners * cap, half), BF),
        jax.ShapeDtypeStruct((128, cap), F32),
        jax.ShapeDtypeStruct((8, block), F32),
        jax.ShapeDtypeStruct((block, 128), F32),
    )
    return run(
        pick_kernel, "pick", 9, (dp,), (ids, table), (1,),
        [whole(ids.shape), whole(table.shape)],
        [whole(s.shape) for s in shapes],
        shapes,
        [pltpu.VMEM((owners, block), jnp.int32)] * 2 + [pltpu.VMEM((group * cap, rows), BF)],
    )


def regather_kernel(col_ref, got_ref, own_ref, send_ref):
    slots = got_ref.shape[0]
    half = own_ref.shape[0]
    for part, out in ((1, send_ref), (0, own_ref)):
        slot = col_ref[part * half : (part + 1) * half, 0:1].astype(jnp.int32)
        hot = (iota((half, slots), 1) == slot).astype(F32).astype(BF)
        out[...] = dot_nn(hot, got_ref[...]).astype(BF)


def regather(col, got, after):
    block, half = col.shape[0], got.shape[1]
    shapes = [jax.ShapeDtypeStruct((block // 2, half), BF)] * 2
    return run(
        regather_kernel, "regather", 2.5, (), (col, got), (1,),
        [whole(col.shape), whole(got.shape)], [whole(s.shape) for s in shapes], shapes, (), after,
    )


def spread_kernel(row_ref, own_ref, other_ref, out_ref):
    half = own_ref.shape[0]
    step = out_ref.shape[0]
    base = pl.program_id(0) * step
    slot = row_ref[0:1, :].astype(jnp.int32)
    place = iota((step, half), 0) + base
    hot_own = (place == slot[:, :half]).astype(F32).astype(BF)
    hot_other = (place == slot[:, half:]).astype(F32).astype(BF)
    out_ref[...] = (dot_nn(hot_own, own_ref[...]) + dot_nn(hot_other, other_ref[...])).astype(BF)


def spread(row, own, other, slots, after):
    step = 512
    return run(
        spread_kernel, "spread", 3.7, (), (row, own, other), (slots // step,),
        [whole(row.shape), whole(own.shape), whole(other.shape)],
        pl.BlockSpec((step, own.shape[1]), lambda i: (i, 0)),
        jax.ShapeDtypeStruct((slots, own.shape[1]), BF),
        (),
        after,
    )


def table_kernel(asked_ref, got_ref, out_ref):
    step = out_ref.shape[0]
    base = pl.program_id(0) * step
    total = jnp.zeros(out_ref.shape, F32)
    lines, width = asked_ref.shape
    for c in range(lines):
        asked = asked_ref[c : c + 1, :].astype(jnp.int32)
        hot = (iota((step, width), 0) + base == asked).astype(F32).astype(BF)
        total = total + dot_nn(hot, got_ref[c * width : (c + 1) * width, :])
    out_ref[...] = total


def table_grad(asked, got, rows, after):
    step = 640 if rows % 640 == 0 else rows
    return run(
        table_kernel, "table_grad", 5.5, (), (asked, got), (rows // step,),
        [whole(asked.shape), whole(got.shape)],
        pl.BlockSpec((step, got.shape[1]), lambda i: (i, 0)),
        jax.ShapeDtypeStruct((rows, got.shape[1]), F32),
        (),
        after,
    )


def pair_of(i, s, count):
    return jnp.where(i < count, s[0] * count + i, (1 - s[0]) * count + i - count)


def head_views(key, query, length):
    lane = iota(query.shape, 1)
    dead = jnp.where(iota(key.shape, 0) < length, 0.0, -1e30).astype(BF)
    one, zero = jnp.ones_like(query), jnp.zeros_like(query)
    for h in range(2):
        spare = HDIM if h == 0 else 0
        this = (lane < HDIM) if h == 0 else (lane >= HDIM)
        yield this, jnp.where(lane == spare, dead, key), jnp.where(this, query, jnp.where(lane == spare, one, zero))


def attend_kernel(place, own_ref, other_ref, mine_ref, theirs_ref, emb_ref, proj_ref, out_ref, stat_ref):
    half = own_ref.shape[1]
    step = pl.program_id(0)

    @pl.when(step == 0)
    def _():
        @pl.when(place[0] == 0)
        def _():
            emb_ref[:, :half] = own_ref[...]
            emb_ref[:, half:] = other_ref[...]

        @pl.when(place[0] != 0)
        def _():
            emb_ref[:, :half] = other_ref[...]
            emb_ref[:, half:] = own_ref[...]

    weight = jnp.where(step < half // 128, mine_ref[...], theirs_ref[...])
    weight = jnp.concatenate([weight[0], weight[1], weight[2]], axis=1)
    proj = dot_nn(emb_ref[...], weight).astype(BF)
    query, key, value = proj[:, :128], proj[:, 128:256], proj[:, 256:]
    proj_ref[0] = query
    proj_ref[1] = key
    proj_ref[2] = value
    value_t = jnp.transpose(value)
    parts = []
    for h, (_, keys, queries) in enumerate(head_views(key, query, place[1])):
        score = dot_nt(keys, queries)
        top = jnp.max(score, axis=0, keepdims=True) * (0.125 * LOG2E)
        power = jnp.exp2(score * (0.125 * LOG2E) - top)
        total = jnp.sum(power, axis=0, keepdims=True)
        stat_ref[0, h : h + 1, :] = top + jnp.log2(total)
        parts.append(dot_nn(value_t[h * HDIM : (h + 1) * HDIM], power.astype(BF)) * (1.0 / total))
    out_ref[...] = jnp.transpose(jnp.concatenate(parts, axis=0)).astype(BF)


def attend(place, own, other, mine, theirs):
    seq, half = own.shape
    width = 2 * half
    pairs = width // 128
    count = pairs // 2
    shapes = (
        jax.ShapeDtypeStruct((seq, width), BF),
        jax.ShapeDtypeStruct((3, seq, width), BF),
        jax.ShapeDtypeStruct((seq, width), BF),
        jax.ShapeDtypeStruct((pairs, 8, seq), F32),
    )
    return run(
        attend_kernel, "attend", 12, (place,), (own, other, mine, theirs), (pairs,),
        [
            whole(own.shape),
            whole(other.shape),
            pl.BlockSpec((3, width, 128), lambda i, s: (0, 0, jnp.minimum(i, count - 1))),
            pl.BlockSpec((3, width, 128), lambda i, s: (0, 0, jnp.maximum(i - count, 0))),
        ],
        [
            whole((seq, width)),
            pl.BlockSpec((3, seq, 128), lambda i, s: (0, 0, i)),
            pl.BlockSpec((seq, 128), lambda i, s: (0, pair_of(i, s, count))),
            pl.BlockSpec((1, 8, seq), lambda i, s: (i, 0, 0)),
        ],
        shapes,
    )


def attend_back_kernel(last, place, proj_ref, grad_ref, stat_ref, weight_ref, sum_ref, gproj_ref, *outs):
    step = pl.program_id(0)
    query, key, value = proj_ref[0], proj_ref[1], proj_ref[2]
    grad = grad_ref[...]
    lane = iota(query.shape, 1)
    key_t = jnp.transpose(key)
    queries_t, grads_k, grads_v = [], [], []
    for h, (this, keys, queries) in enumerate(head_views(key, query, place[1])):
        score = dot_nt(keys, queries)
        probs = jnp.exp2(score * (0.125 * LOG2E) - stat_ref[0, h : h + 1, :])
        grads_v.append(dot_nn(probs.astype(BF), grad))
        grad_probs = dot_nt(value, jnp.where(this, grad, jnp.zeros_like(grad)))
        dots = jnp.sum(probs * grad_probs, axis=0, keepdims=True)
        grad_raw = (probs * (grad_probs - dots)).astype(BF)
        grads_k.append(dot_nn(grad_raw, query))
        queries_t.append(dot_nn(key_t[h * HDIM : (h + 1) * HDIM], grad_raw))
    grad_query = (jnp.transpose(jnp.concatenate(queries_t, axis=0)) * 0.125).astype(BF)
    grad_key = (jnp.where(lane < HDIM, grads_k[0], grads_k[1]) * 0.125).astype(BF)
    grad_value = jnp.where(lane < HDIM, grads_v[0], grads_v[1]).astype(BF)
    gproj_ref[0] = grad_query
    gproj_ref[1] = grad_key
    gproj_ref[2] = grad_value
    weight = weight_ref[...]
    weight = jnp.concatenate([weight[0], weight[1], weight[2]], axis=1)
    more = dot_nt(jnp.concatenate([grad_query, grad_key, grad_value], axis=1), weight)
    total = outs[-1]

    @pl.when(step == 0)
    def _():
        total[...] = sum_ref[...] + more

    @pl.when(step > 0)
    def _():
        total[...] += more

    if last:
        own_ref, send_ref = outs[:2]
        half = own_ref.shape[1]

        @pl.when(step == pl.num_programs(0) - 1)
        def _():
            low = total[...].astype(BF)

            @pl.when(place[0] == 0)
            def _():
                own_ref[...] = low[:, :half]
                send_ref[...] = low[:, half:]

            @pl.when(place[0] != 0)
            def _():
                own_ref[...] = low[:, half:]
                send_ref[...] = low[:, :half]


def attend_back(place, proj, grad, stat, weight, grad_sum, mine, after):
    seq, width = grad.shape
    half = width // 2
    count = half // 128
    base = 0 if mine else count
    gproj = jax.ShapeDtypeStruct((3, seq, half), BF)
    part = jax.ShapeDtypeStruct((seq, half), BF)
    total = jax.ShapeDtypeStruct((seq, width), F32)
    out_specs = [pl.BlockSpec((3, seq, 128), lambda i, s: (0, 0, i))]
    return run(
        functools.partial(attend_back_kernel, mine), "attend_back", 9, (place,),
        (proj, grad, stat, weight, grad_sum), (count,),
        [
            pl.BlockSpec((3, seq, 128), lambda i, s: (0, 0, i + base)),
            pl.BlockSpec((seq, 128), lambda i, s: (0, pair_of(i + base, s, count))),
            pl.BlockSpec((1, 8, seq), lambda i, s: (i + base, 0, 0)),
            pl.BlockSpec((3, width, 128), lambda i, s: (0, 0, i)),
            whole((seq, width)),
        ],
        out_specs + ([whole(part.shape)] * 2 if mine else [whole(total.shape)]),
        [gproj] + ([part] * 2 if mine else [total]),
        [pltpu.VMEM((seq, width), F32)] if mine else [],
        after,
    )


def gelu_parts(x):
    size = jnp.abs(x)
    t = 1.0 / (1.0 + (0.3275911 * 0.7071067811865476) * size)
    bell = jnp.exp2(x * x * (-0.5 * LOG2E))
    poly = t * (0.254829592 + t * (-0.284496736 + t * (1.421413741 + t * (-1.453152027 + t * 1.061405429))))
    tail = 0.5 * poly * bell
    phi_sum = jnp.where(x >= 0, 1.0 - tail, tail)
    return x * phi_sum, phi_sum + x * bell * 0.3989422804014327


def norm_parts(v):
    centre = v - jnp.mean(v, axis=-1, keepdims=True)
    spread_of = jnp.mean(centre * centre, axis=-1, keepdims=True)
    scale = lax.rsqrt(spread_of + 1e-12)
    return centre * scale, scale


def norm_back(grad, normal, scale, gain):
    e = grad * gain
    return scale * (e - jnp.mean(e, -1, keepdims=True) - normal * jnp.mean(e * normal, -1, keepdims=True))


def forward_kernel(
    place, att_ref, emb_ref, out_w_ref, vec_ref, cot_ref, in_ref, back_ref,
    low_ref, normal_ref, scale_ref, send_ref, keep_ref, slope_ref, mixed_ref, outer_ref, weights_ref, sums_ref,
):
    step = pl.program_id(0)
    half_steps = pl.num_programs(0) // 2
    seq = att_ref.shape[0]

    @pl.when(step == 0)
    def _():
        total = emb_ref[...].astype(F32) + dot_nn(att_ref[...], out_w_ref[...])
        normal, scale = norm_parts(total)
        normed = normal * vec_ref[0:1, :] + vec_ref[1:2, :]
        normal_ref[...] = normal
        scale_ref[...] = jnp.broadcast_to(scale, scale_ref.shape)
        low_ref[...] = normed.astype(BF)
        mixed_ref[...] = normed

    inner = dot_nt(low_ref[...], in_ref[...])
    active, slope = gelu_parts(inner)
    active = active.astype(BF)
    slope_ref[...] = slope

    @pl.when(step < half_steps)
    def _():
        send_ref[...] = active

    @pl.when(step >= half_steps)
    def _():
        keep_ref[...] = active

    mixed_ref[...] += dot_nn(active, back_ref[...])

    @pl.when(step == pl.num_programs(0) - 1)
    def _():
        normal, scale = norm_parts(mixed_ref[...])
        gain, term = vec_ref[2:3, :], vec_ref[3:4, :]
        final = normal * gain
        logit = jnp.sum(final * term, axis=-1, keepdims=True)
        live = (iota((seq, 1), 0) < place[1]).astype(F32)
        rest = jnp.exp(-jnp.abs(logit))
        weights = (jnp.maximum(logit, 0.0) + jnp.log1p(rest)) * live
        weights_ref[...] = jnp.broadcast_to(weights, weights_ref.shape)
        sigmoid = jnp.where(logit >= 0, 1.0, rest) / (1.0 + rest)
        grad_logit = cot_ref[:, 0:1] * live * sigmoid
        grad_final = grad_logit * term
        sums_ref[0:1, :] = jnp.sum(grad_final * normal, axis=0, keepdims=True)
        sums_ref[1:2, :] = jnp.sum(grad_logit * final, axis=0, keepdims=True)
        sums_ref[2:8, :] = jnp.zeros((6, sums_ref.shape[1]), F32)
        grad_mixed = norm_back(grad_final, normal, scale, gain)
        mixed_ref[...] = grad_mixed
        outer_ref[...] = grad_mixed.astype(BF)


def forward(place, att, emb, out_w, vec, cot, in_rows, back_rows):
    seq, width = att.shape
    units = in_rows.shape[0]
    step = 768
    count = units // step
    part = count // 2
    shapes = (
        jax.ShapeDtypeStruct((seq, width), BF),
        jax.ShapeDtypeStruct((seq, width), F32),
        jax.ShapeDtypeStruct((seq, 128), F32),
        jax.ShapeDtypeStruct((seq, units // 2), BF),
        jax.ShapeDtypeStruct((seq, units // 2), BF),
        jax.ShapeDtypeStruct((seq, units), F32),
        jax.ShapeDtypeStruct((seq, width), F32),
        jax.ShapeDtypeStruct((seq, width), BF),
        jax.ShapeDtypeStruct((seq, 128), F32),
        jax.ShapeDtypeStruct((8, width), F32),
    )
    return run(
        forward_kernel, "forward", 17, (place,), (att, emb, out_w, vec, cot, in_rows, back_rows), (count,),
        [
            whole((seq, width)),
            whole((seq, width)),
            whole((width, width)),
            whole(vec.shape),
            whole(cot.shape),
            pl.BlockSpec((step, width), lambda i, s: (lax.rem(i + part, count), 0)),
            pl.BlockSpec((step, width), lambda i, s: (lax.rem(i + part, count), 0)),
        ],
        [
            whole((seq, width)),
            whole((seq, width)),
            whole((seq, 128)),
            pl.BlockSpec((seq, step), lambda i, s: (0, jnp.minimum(i, part - 1))),
            pl.BlockSpec((seq, step), lambda i, s: (0, jnp.maximum(i - part, 0))),
            pl.BlockSpec((seq, step), lambda i, s: (0, lax.rem(i + part, count))),
            whole((seq, width)),
            whole((seq, width)),
            whole((seq, 128)),
            whole((8, width)),
        ],
        shapes,
    )


def backward_kernel(last, outer_ref, start_ref, slope_ref, in_ref, back_ref, *refs):
    step = pl.program_id(0)
    if last:
        normal_ref, scale_ref, out_w_ref, vec_ref, inner_ref, total_ref, branch_ref, att_ref, sums_ref = refs
    else:
        inner_ref, total_ref = refs
    grad_inner = (dot_nt(outer_ref[...], back_ref[...]) * slope_ref[...]).astype(BF)
    inner_ref[...] = grad_inner
    more = dot_nn(grad_inner, in_ref[...])

    @pl.when(step == 0)
    def _():
        total_ref[...] = start_ref[...] + more

    @pl.when(step > 0)
    def _():
        total_ref[...] += more

    if last:

        @pl.when(step == pl.num_programs(0) - 1)
        def _():
            grad = total_ref[...]
            normal = normal_ref[...]
            sums_ref[0:1, :] = jnp.sum(grad * normal, axis=0, keepdims=True)
            sums_ref[1:2, :] = jnp.sum(grad, axis=0, keepdims=True)
            sums_ref[2:8, :] = jnp.zeros((6, sums_ref.shape[1]), F32)
            grad_sum = norm_back(grad, normal, scale_ref[:, 0:1], vec_ref[0:1, :])
            total_ref[...] = grad_sum
            branch = grad_sum.astype(BF)
            branch_ref[...] = branch
            att_ref[...] = dot_nt(branch, out_w_ref[...]).astype(BF)


def backward(outer, start, slope, in_rows, back_rows, rest, after):
    seq, width = outer.shape
    units = in_rows.shape[0]
    step = 768
    count = units // step // 2
    base = 0 if rest else count
    shapes = [jax.ShapeDtypeStruct((seq, units // 2), BF), jax.ShapeDtypeStruct((seq, width), F32)]
    if rest:
        shapes += [jax.ShapeDtypeStruct((seq, width), BF)] * 2 + [jax.ShapeDtypeStruct((8, width), F32)]
    return run(
        functools.partial(backward_kernel, bool(rest)), "backward", 7, (),
        (outer, start, slope, in_rows, back_rows) + tuple(rest), (count,),
        [
            whole((seq, width)),
            whole((seq, width)),
            pl.BlockSpec((seq, step), lambda i: (0, i + base)),
            pl.BlockSpec((step, width), lambda i: (i + base, 0)),
            pl.BlockSpec((step, width), lambda i: (i + base, 0)),
        ]
        + [whole(r.shape) for r in rest],
        [pl.BlockSpec((seq, step), lambda i: (0, i))] + [whole(x.shape) for x in shapes[1:]],
        shapes,
        (),
        after,
    )


def unit_grad_kernel(own_ref, recv_ref, own_other, recv_other, low_ref, high_ref):
    rows = low_ref.shape[0]
    for i, out in enumerate((high_ref, low_ref)):
        cols = slice((1 - i) * rows, (2 - i) * rows)
        out[...] = (dot_tn(own_ref[:, cols], own_other[...]) + dot_tn(recv_ref[:, cols], recv_other[...])).astype(BF)


def unit_grad(own, recv, own_other, recv_other, after):
    width = own_other.shape[1]
    shape = jax.ShapeDtypeStruct((own.shape[1] // 2, width), BF)
    args = (own, recv, own_other, recv_other)
    return run(
        unit_grad_kernel, "unit_grad", 3, (), args, (1,),
        [whole(a.shape) for a in args], [whole(shape.shape)] * 2, [shape] * 2, (), after,
    )


def side_grad_kernel(
    order_ref, spots_ref, emb_ref, emb_recv, gproj_ref, gproj_recv, branch_ref, branch_recv, att_ref, att_recv,
    sums_ref, sums_recv, low_ref, high_ref,
):
    seq, width = att_ref.shape
    half = width // 2
    rows = half // 2
    outs = (low_ref, high_ref)
    for k in range(2):
        place = order_ref[0:1, k * half : (k + 1) * half]
        hot = (iota((width, half), 0) == place).astype(F32).astype(BF)
        moved = dot_nn(emb_ref[...], hot).astype(BF)
        moved_recv = dot_nn(emb_recv[...], hot).astype(BF)
        for c in range(3):
            grad = (dot_tn(moved, gproj_ref[c]) + dot_tn(moved_recv, gproj_recv[c])).astype(BF)
            at = (3 * k + c) * half
            low_ref[:, at : at + half] = grad[:rows]
            high_ref[:, at : at + half] = grad[rows:]
    hot = (iota((width, half), 0) == spots_ref[0:1, :]).astype(F32).astype(BF)
    moved = dot_nn(branch_ref[...], hot).astype(BF)
    moved_recv = dot_nn(branch_recv[...], hot).astype(BF)
    grad = (dot_tn(moved, att_ref[...]) + dot_tn(moved_recv, att_recv[...])).astype(BF)
    lines = jnp.concatenate([sums_ref[...] + sums_recv[...], jnp.zeros((112, width), F32)], axis=0).astype(BF)
    sums = jnp.transpose(dot_nn(lines, hot)).astype(BF)
    for i, out in enumerate(outs):
        out[:, 6 * half : 8 * half] = grad[i * rows : (i + 1) * rows]
        out[:, 8 * half :] = sums[i * rows : (i + 1) * rows]


def side_grad(*args, after):
    width = args[2].shape[1]
    half = width // 2
    shapes = [jax.ShapeDtypeStruct((half // 2, 8 * half + 128), BF)] * 2
    return run(
        side_grad_kernel, "side_grad", 6, (), args, (1,),
        [whole(a.shape) for a in args], [whole(x.shape) for x in shapes], shapes, (), after,
    )


def swap_head(x):
    return lax.ppermute(x, "head", [(0, 1), (1, 0)])


def swap_dp(x, bit):
    return lax.ppermute(x, "dp", [(i, i ^ bit) for i in range(lax.axis_size("dp"))])


def swap_both(x, bits):
    count = lax.axis_size("dp")
    pairs = [(2 * i + h, 2 * (i ^ bits[h]) + h) for i in range(count) for h in range(2)]
    return lax.ppermute(x, ("dp", "head"), pairs)


def add_kernel(keep_low, keep_high, recv_low, recv_high, send, keep):
    send[...] = keep_high[...] + recv_high[...]
    keep[...] = keep_low[...] + recv_low[...]


def add_halves(keep, recv, after=()):
    if isinstance(keep, tuple):
        half, width = keep[0].shape
    else:
        half, width = keep.shape[0] // 2, keep.shape[1]
        if half % 16:
            total = keep + recv
            return total[half:], total[:half]
    steps = 2 if half % 32 == 0 and half >= 384 else 1
    block = half // steps
    low = pl.BlockSpec((block, width), lambda i: (i, 0))
    high = pl.BlockSpec((block, width), lambda i: (i + steps, 0))
    args, specs = [], []
    for x in (keep, recv):
        args += list(x) if isinstance(x, tuple) else [x, x]
        specs += [low, low] if isinstance(x, tuple) else [low, high]
    shape = jax.ShapeDtypeStruct((half, width), BF)
    return run(add_kernel, "add_halves", 1, (), args, (steps,), specs, [low, low], [shape, shape], (), after)


class Sum:
    def __init__(self, bits, low, high):
        self.bits, self.keep, self.done = bits, low, 0
        self.swap(high)

    def swap(self, send):
        k = self.done
        if k < 2:
            self.recv = swap_both(send, (self.bits[0], self.bits[1]) if k == 0 else (self.bits[1], self.bits[0]))
        else:
            self.recv = swap_dp(send, self.bits[k])
        self.done += 1

    def step(self, after=()):
        send, self.keep = add_halves(self.keep, self.recv, after)
        self.swap(send)
        return self.keep

    def result(self):
        return self.keep.astype(F32) + self.recv.astype(F32)


def reversed_bits(count):
    bits = count.bit_length() - 1
    return [sum(((i >> b) & 1) << (bits - 1 - b) for b in range(bits)) for i in range(count)]


def swap_low(i):
    return (i & ~3) | ((i & 1) << 1) | ((i >> 1) & 1)


def body(
    token_ids,
    lengths,
    embed_table,
    qkv_weight,
    out_weight,
    first_gain,
    first_bias,
    in_weight,
    back_weight,
    second_gain,
    term_vector,
    cotangent,
):
    dp = lax.axis_index("dp")
    head = lax.axis_index("head")
    owners = lax.axis_size("dp")
    bits = [1 << b for b in range(owners.bit_length() - 1)]
    device = dp * 2 + head
    seq = token_ids.shape[0]
    table_rows, half = embed_table.shape
    width = 2 * half
    units = back_weight.shape[0]
    cap = 4 * seq // owners
    slots = owners * cap

    ids = token_ids.reshape(1, seq)
    ids = jnp.concatenate([ids, swap_head(ids)], axis=1)
    for low, high in zip(bits[::2], bits[1::2] + [0]):
        parts = [swap_dp(ids, b) for b in ((low, high, low + high) if high else (low,))]
        ids = jnp.concatenate([ids] + parts, axis=0)
    picked, asked, slot_row, slot_col = pick(dp.reshape(1), ids, embed_table, cap)
    got = lax.all_to_all(picked.reshape(owners, cap, half), "dp", split_axis=0, concat_axis=0, tiled=True)

    rev = reversed_bits(owners)
    ways = jnp.array([rev, [swap_low(r) for r in rev]], jnp.int32)
    keep_blocks, send_blocks = (ways[head] ^ dp) * 2 + head, (ways[1 - head] ^ dp) * 2 + 1 - head
    unit_order = jnp.concatenate([keep_blocks, send_blocks])
    back_rows = jnp.take(back_weight.reshape(2 * owners, -1, width), unit_order, axis=0, mode="clip").reshape(units, width)
    in_rows = jnp.take(in_weight.T.reshape(2 * owners, -1, width), unit_order, axis=0, mode="clip").reshape(units, width)
    other_weight = swap_head(qkv_weight)
    out_block = width // (2 * owners)
    inside = jnp.arange(out_block, dtype=jnp.int32)[None, :]
    lines = lambda start: (start[:, None] * out_block + inside).reshape(1, half)
    spots = lines(keep_blocks)
    order = jnp.concatenate([lines(keep_blocks - head), lines(keep_blocks - head + 1)], axis=1)
    vec = jnp.concatenate(
        [jnp.stack([first_gain, first_bias, second_gain, term_vector]), jnp.zeros((4, width), F32)], axis=0
    )
    asked_rows = asked[:owners].reshape(slots // 512, 512)
    cot = jnp.broadcast_to(cotangent.reshape(seq, 1), (seq, 128))
    place = jnp.stack([head, lengths[0]]).astype(jnp.int32)

    own, send = regather(
        slot_col, got.reshape(slots, half),
        (in_rows, back_rows, other_weight, vec, cot, spots, order, asked_rows),
    )
    other = swap_head(send)
    emb, proj, att, stat = attend(place, own, other, qkv_weight, other_weight)
    emb_recv, att_recv = swap_head(emb), swap_head(att)
    low, normal, scale, active_send, active, slope, mixed, outer, weights, sums_two = forward(
        place, att, emb, out_weight, vec, cot, in_rows, back_rows
    )
    low_recv, outer_recv, active_recv = swap_head(low), swap_head(outer), swap_head(active_send)
    inner_send, total = backward(outer, mixed, slope, in_rows, back_rows, (), ())
    inner_recv = swap_head(inner_send)
    back = Sum(bits, *unit_grad(active, active_recv, outer, outer_recv, (total,)))
    inner, grad_sum, branch, grad_att, sums_one = backward(
        outer, total, slope, in_rows, back_rows, (normal, scale, out_weight, vec), (back.keep,)
    )
    sums = jnp.concatenate([sums_one, sums_two], axis=0)
    branch_recv, sums_recv = swap_head(branch), swap_head(sums)
    ins = Sum(bits, *unit_grad(inner, inner_recv, low, low_recv, (grad_sum,)))
    gproj_send, total = attend_back(place, proj, grad_att, stat, other_weight, grad_sum, False, (ins.keep,))
    gproj_recv = swap_head(gproj_send)
    t = back.step((total,))
    gproj, grad_own, grad_send = attend_back(place, proj, grad_att, stat, qkv_weight, total, True, (t,))
    grad_other = swap_head(grad_send)
    t = back.step((grad_own,))
    t = ins.step((t,))
    sent = spread(slot_row, grad_own, grad_other, slots, (t,))
    arrived = lax.all_to_all(sent.reshape(owners, cap, half), "dp", split_axis=0, concat_axis=0, tiled=True)
    side = Sum(
        bits,
        *side_grad(
            order, spots, emb, emb_recv, gproj, gproj_recv, branch, branch_recv, att, att_recv, sums, sums_recv,
            after=(sent,),
        ),
    )
    t = back.step((side.keep,))
    t = ins.step((t,))
    t = side.step((t,))
    t = ins.step((t,))
    while ins.done < len(bits):
        t = ins.step((t,))
    while back.done < len(bits):
        t = back.step((t,))
    grad_table = table_grad(asked_rows, arrived.reshape(slots, half), table_rows, (t,))
    t = grad_table
    while side.done < len(bits):
        t = side.step((t,))
    grad_back, grad_in, side = back.result(), ins.result(), side.result()
    grad_out = side[:, 6 * half : 8 * half]
    grad_qkv = jnp.concatenate([side[:, : 3 * half], side[:, 3 * half : 6 * half]], axis=0)
    grad_qkv = grad_qkv.reshape(-1, 3, half).transpose(1, 0, 2)
    vectors = side[:, 8 * half :]
    return (
        weights[:, 0],
        grad_table,
        grad_qkv,
        grad_out.T,
        grad_in.T,
        grad_back,
        vectors[:, 0],
        vectors[:, 1],
        vectors[:, 8],
        vectors[:, 9],
    )


def solution(mesh):
    in_specs = (
        P(("dp", "head")),
        P(("dp", "head")),
        P("dp", "head"),
        P(None, None, "head"),
        P(),
        P(),
        P(),
        P(),
        P(),
        P(),
        P(),
        P(("dp", "head")),
    )
    out_specs = (
        P(("dp", "head")),
        P("dp", "head"),
        P(None, "dp", "head"),
        P(None, ("dp", "head")),
        P(None, ("dp", "head")),
        P(("dp", "head"), None),
        P(("dp", "head")),
        P(("dp", "head")),
        P(("dp", "head")),
        P(("dp", "head")),
    )
    return jax.shard_map(body, mesh=mesh, in_specs=in_specs, out_specs=out_specs, check_vma=False)
```

time: 324 us -> 270 us (0.83)
  waiting for transfers between devices: 100 us -> 65.5 us
  other arithmetic: 30 us -> 6.28 us
  local copies, waits for them, and re-layouts: 32.3 us -> 51 us
  Pallas kernels: 109 us -> 99 us
  starting transfers between devices: 49.6 us -> 42.4 us
    ppermute x24 -> x12, waiting for transfers between devices: 94.8 us -> 39.2 us  [swap_dp(): lax.ppermute(x, 'dp', [(i, i ^ bit) for i in range(lax.axis_size('dp'))])]
    ppermute x24 -> x12, starting transfers between devices: 36.4 us -> 19.1 us  [swap_dp(): lax.ppermute(x, 'dp', [(i, i ^ bit) for i in range(lax.axis_size('dp'))])]
    ppermute x0 -> x6, waiting for transfers between devices: none -> 15.8 us  [swap_both(): return lax.ppermute(x, ('dp', 'head'), pairs)]
    select_n x2 -> x0, other arithmetic: 13.1 us -> none  [the longest x1 8.27 us: body(): jnp.take(back_weight.reshape(2 * owners, -1, width), unit_order, axis=0)]
    unnamed x60 -> x96, local copies, waits for them, and re-layouts: 15.9 us -> 28.1 us
    pallas_call x12 -> x21, Pallas kernels: 109 us -> 99 us  [run(): pl.pallas_call(inner, grid_spec=pltpu.PrefetchScalarGridSpec(num_scalar_p...]
    add x27 -> x5, other arithmetic: 12.4 us -> 2.92 us  [the longest x2 2.07 us: body(): lines = lambda start: (start[:, None] * out_block + inside).reshape(1, half)]
    ppermute x0 -> x6, starting transfers between devices: none -> 8.35 us  [swap_both(): return lax.ppermute(x, ('dp', 'head'), pairs)]
  transfers between devices with their start and end apart: 34 -> 33, of which waited for: 20 -> 20; matrix products, arithmetic and copies ran while one was open for 15% -> 12% of each run, Pallas kernels for 15% -> 21%
where the time goes in v2:
time: 270 us; the launch traced here: 266 us
  Pallas kernels  99 us (37%)
  waiting for transfers between devices  65.5 us (24%)
  local copies, waits for them, and re-layouts  51 us (19%)
  starting transfers between devices  42.4 us (16%)
  other arithmetic  6.28 us (2%)
    pallas_call x21, Pallas kernels, run(): pl.pallas_call(inner, grid_spec=pltpu.PrefetchScalarGridSpec(num_scalar_p...  99 us
    ppermute x12, waiting for transfers between devices, swap_dp(): lax.ppermute(x, 'dp', [(i, i ^ bit) for i in range(lax.axis_size('dp'))])  39.2 us
    unnamed x96, local copies, waits for them, and re-layouts  28.1 us
    ppermute x12, starting transfers between devices, swap_dp(): lax.ppermute(x, 'dp', [(i, i ^ bit) for i in range(lax.axis_size('dp'))])  19.1 us
    ppermute x6, waiting for transfers between devices, swap_both(): return lax.ppermute(x, ('dp', 'head'), pairs)  15.8 us
    ppermute x13, waiting for transfers between devices, swap_head(): return lax.ppermute(x, 'head', [(0, 1), (1, 0)])  9.39 us
    ppermute x6, starting transfers between devices, swap_both(): return lax.ppermute(x, ('dp', 'head'), pairs)  8.35 us
    all_to_all x1, starting transfers between devices, body(): lax.all_to_all(sent.reshape(owners, cap, half), 'dp', split_axis=0, conca...  6.78 us
  transfers between devices with their start and end apart: 33, of which 20 were waited for; matrix products, arithmetic and copies ran while one was open for 12% of the time, Pallas kernels for 21%

profile of v2, /device:TPU:0, one launch (start us, length us, event | category | flops | bytes accessed | tf_op | source)
XLA Modules:
  0.0 266.4 jit_solution(504228583827727247)
XLA Ops:
  23.6 8.3 %pick.1 = (bf16[2048,384]{1,0:T(8,128)(2,1)}, f32[128,128]{1,0:T(8,128)S(1)}, f32[8,1024]{1,0:T(8,128)S(1)}, f32[1024,128]{1,0:T(8,128)S(1)}) custom-call(s32[1]{0:T(128)} %bitcast.1.refs_0_, s32[16,1024]{1,0:T(8,128)S(1)} %concatenate.27.refs_1_, bf16[1920,384]{1,0:T(8,128)(2,1)S(1)} %copy-done.14), custom_call_target="tpu_custom_call" | custom-call | bytes 9000 | tf_op jit(solution)/shard_map/pick/pallas_call | solution.py:54
  34.0 4.7 %all-to-all-start = ((bf16[16,128,384]{2,1,0:T(8,128)(2,1)}), bf16[16,128,384]{2,1,0:T(8,128)(2,1)}, u32[]{:S(2)}, u32[]{:S(2)}) async-start(bf16[16,128,384]{2,1,0:T(8,128)(2,1)} %bitcast.3), calls=%async_computation | async-start | bytes 3145728 | tf_op jit(solution)/shard_map/all_to_all | solution.py:692
  38.8 6.7 %copy.24 = bf16[768,3072]{0,1:T(8,128)(2,1)} copy(bf16[768,3072]{1,0:T(8,128)(2,1)} %param.20) | data formatting | bytes 9437184 | tf_op args[7]
  46.7 5.3 %gather_fusion = bf16[32,96,768]{2,1,0:T(8,128)(2,1)} fusion(bf16[32,96,768]{2,1,0:T(8,128)(2,1)} %bitcast.38, s32[1024]{0:T(1024)S(1)} %pad_clamp_fusion), kind=kCustom, calls=%fused_computation | custom fusion | bytes 9437312 | tf_op jit(solution)/shard_map/jit(_take)/gather | solution.py:699
  52.0 5.3 %gather_fusion.1 = bf16[32,96,768]{2,1,0:T(8,128)(2,1)} fusion(bf16[32,96,768]{2,1,0:T(8,128)(2,1)} %bitcast.39, s32[1024]{0:T(1024)S(1)} %pad_clamp_fusion), kind=kCustom, calls=%fused_computation.1 | custom fusion | bytes 9437312 | tf_op jit(solution)/shard_map/jit(_take)/gather | solution.py:698
  77.6 3.8 %regather.1 = (bf16[512,384]{1,0:T(8,128)(2,1)S(1)}, bf16[512,384]{1,0:T(8,128)(2,1)S(1)}) custom-call(f32[1024,128]{1,0:T(8,128)S(1)} %copy-done.20, bf16[2048,384]{1,0:T(8,128)(2,1)} %bitcast.4.refs_1_, bf16[3072,768]{1,0:T(8,128)(2,1)S(1)} %bitcast.29, bf16[3072,768]{1,0:T(8,128)(2,1)S(1)} %bitcast.36, ...), custom_call_target="tpu_custom_call" | custom-call | bytes 2500 | tf_op jit(solution)/shard_map/regather/pallas_call | solution.py:54
  83.2 12.2 %attend.1 = (bf16[512,768]{1,0:T(8,128)(2,1)S(1)}, bf16[3,512,768]{2,1,0:T(8,128)(2,1)S(1)}, bf16[512,768]{1,0:T(8,128)(2,1)S(1)}, f32[6,8,512]{2,1,0:T(8,128)S(1)}) custom-call(s32[2]{0:T(128)S(1)} %pad_add_fusion.2.refs_0_, bf16[512,384]{1,0:T(8,128)(2,1)S(1)} %get-tuple-element.67.refs_1_, bf16[512,384]{1,0:T(8,128)(2,1)S(1)} %collective-permute-done.8.refs_2_, ...), custom_call_target="tpu_custom_call" | custom-call | bytes 12000 | tf_op jit(solution)/shard_map/attend/pallas_call | solution.py:54
  96.1 19.3 %forward.1 = (bf16[512,768]{1,0:T(8,128)(2,1)S(1)}, f32[512,768]{1,0:T(8,128)S(1)}, f32[512,128]{1,0:T(8,128)S(1)}, bf16[512,1536]{1,0:T(8,128)(2,1)}, bf16[512,...) custom-call(s32[2]{0:T(128)S(1)} %pad_add_fusion.2.refs_0_, ...), custom_call_target="tpu_custom_call" | custom-call | bytes 17000 | tf_op jit(solution)/shard_map/forward/pallas_call | solution.py:54
  117.4 5.8 %backward.2 = (bf16[512,1536]{1,0:T(8,128)(2,1)S(1)}, f32[512,768]{1,0:T(8,128)S(1)}) custom-call(bf16[512,768]{1,0:T(8,128)(2,1)S(1)} %get-tuple-element.74.refs_0_.refs_2_, f32[512,768]{1,0:T(8,128)S(1)} %get-tuple-element.75.refs_1_, f32[512,3072]{1,0:T(8,128)} %get-tuple-element.76.refs_2_, bf16[3072,768]{1,0:T(8,128)(2,1)S(1)} %bitcast.32, ...), custom_call_target="tpu_custom_call" | custom-call | bytes 7000 | tf_op jit(solution)/shard_map/backward/pallas_call | solution.py:54
  124.2 3.7 %collective-permute-done.10.refs_3_ = bf16[512,768]{1,0:T(8,128)(2,1)S(1)} collective-permute-done((bf16[512,768]{1,0:T(8,128)(2,1)S(1)}, bf16[512,768]{1,0:T(8,128)(2,1)S(1)}, u32[]{:S(2)}, u32[]{:S(2)}) %collective-permute-start.10) | collective-permute-done | bytes 786464 | tf_op jit(solution)/shard_map/ppermute | solution.py:591
  131.8 7.3 %backward.3 = (bf16[512,1536]{1,0:T(8,128)(2,1)S(1)}, f32[512,768]{1,0:T(8,128)S(1)}, bf16[512,768]{1,0:T(8,128)(2,1)S(1)}, bf16[512,768]{1,0:T(8,128)(2,1)S(1)}, f32[8,768]{1,0:T(8,128)S(1)}) custom-call(bf16[512,768]{1,0:T(8,128)(2,1)S(1)} %get-tuple-element.74.refs_0_.refs_2_, f32[512,768]{1,0:T(8,128)S(1)} %get-tuple-element.77.refs_4_.refs_1_, ...), custom_call_target="tpu_custom_call" | custom-call | bytes 7000 | tf_op jit(solution)/shard_map/backward/pallas_call | solution.py:54
  142.7 8.8 %attend_back.2 = (bf16[3,512,384]{2,1,0:T(8,128)(2,1)}, f32[512,768]{1,0:T(8,128)S(1)}) custom-call(s32[2]{0:T(128)S(1)} %copy-done.34, bf16[3,512,768]{2,1,0:T(8,128)(2,1)S(1)} %get-tuple-element.73.refs_1_, bf16[512,768]{1,0:T(8,128)(2,1)S(1)} %get-tuple-element.83.refs_2_, f32[6,8,512]{2,1,0:T(8,128)S(1)} %copy-done.22, ...), custom_call_target="tpu_custom_call" | custom-call | bytes 9000 | tf_op jit(solution)/shard_map/attend_back/pallas_call | solution.py:54
  155.7 8.6 %attend_back.3 = (bf16[3,512,384]{2,1,0:T(8,128)(2,1)S(1)}, bf16[512,384]{1,0:T(8,128)(2,1)S(1)}, bf16[512,384]{1,0:T(8,128)(2,1)S(1)}) custom-call(s32[2]{0:T(128)S(1)} %copy-done.34, bf16[3,512,768]{2,1,0:T(8,128)(2,1)S(1)} %get-tuple-element.73.refs_1_, bf16[512,768]{1,0:T(8,128)(2,1)S(1)} %copy-done.7, f32[6,8,512]{2,1,0:T(8,128)S(1)} %copy-done.22, ...), custom_call_target="tpu_custom_call" | custom-call | bytes 9000 | tf_op jit(solution)/shard_map/attend_back/pallas_call | solution.py:54
  167.9 3.6 %spread.1.refs_12_ = bf16[2048,384]{1,0:T(8,128)(2,1)} custom-call(f32[8,1024]{1,0:T(8,128)S(1)} %copy-done.28, bf16[512,384]{1,0:T(8,128)(2,1)S(1)} %get-tuple-element.93.refs_4_.refs_1_, bf16[512,384]{1,0:T(8,128)(2,1)S(1)} %collective-permute-done.14.refs_2_, bf16[384,768]{1,0:T(8,128)(2,1)S(1)} %get-tuple-element.98.refs_3_.refs_0_.refs_1_), custom_call_target="tpu_custom_call" | custom-call | bytes 3700 | tf_op jit(solution)/shard_map/spread/pallas_call | solution.py:54
  171.5 6.8 %all-to-all-start.1 = ((bf16[16,128,384]{2,1,0:T(8,128)(2,1)}), bf16[16,128,384]{2,1,0:T(8,128)(2,1)S(1)}, u32[]{:S(2)}, u32[]{:S(2)}) async-start(bf16[16,128,384]{2,1,0:T(8,128)(2,1)} %bitcast.14), calls=%async_computation.1 | async-start | bytes 3145728 | tf_op jit(solution)/shard_map/all_to_all | solution.py:741
  186.7 7.6 %side_grad.1 = (bf16[192,3200]{1,0:T(8,128)(2,1)S(1)}, bf16[192,3200]{1,0:T(8,128)(2,1)S(1)}) custom-call(s32[1,768]{1,0:T(1,128)S(1)} %constant_dynamic-update-slice_fusion.refs_8_.refs_0_, s32[1,384]{1,0:T(1,128)S(1)} %add.122.refs_7_.refs_1_, bf16[512,768]{1,0:T(8,128)(2,1)S(1)} %copy-done.9, bf16[512,768]{1,0:T(8,128)(2,1)S(1)} %collective-permute-done.19.refs_3_, ...), custom_call_target="tpu_custom_call" | custom-call | bytes 6000 | tf_op jit(solution)/shard_map/side_grad/pallas_call | solution.py:54
  199.3 13.5 %collective-permute-done.18.refs_2_.refs_3_ = bf16[192,768]{1,0:T(8,128)(2,1)S(1)} collective-permute-done((bf16[192,768]{1,0:T(8,128)(2,1)S(1)}, bf16[192,768]{1,0:T(8,128)(2,1)S(1)}, u32[]{:S(2)}, u32[]{:S(2)}) %collective-permute-start.18) | collective-permute-done | bytes 294944 | tf_op jit(solution)/shard_map/ppermute | solution.py:595
  212.8 4.3 %collective-permute-done.17.refs_2_.refs_3_ = bf16[384,768]{1,0:T(8,128)(2,1)S(1)} collective-permute-done((bf16[384,768]{1,0:T(8,128)(2,1)S(1)}, bf16[384,768]{1,0:T(8,128)(2,1)S(1)}, u32[]{:S(2)}, u32[]{:S(2)}) %collective-permute-start.17) | collective-permute-done | bytes 589856 | tf_op jit(solution)/shard_map/ppermute | solution.py:601
  217.2 10.3 %collective-permute-done.25.refs_2_.refs_3_ = bf16[192,3200]{1,0:T(8,128)(2,1)S(1)} collective-permute-done((bf16[192,3200]{1,0:T(8,128)(2,1)S(1)}, bf16[192,3200]{1,0:T(8,128)(2,1)S(1)}, u32[]{:S(2)}, u32[]{:S(2)}) %collective-permute-start.25) | collective-permute-done | bytes 1228832 | tf_op jit(solution)/shard_map/ppermute | solution.py:601
  229.5 4.9 %collective-permute-start.30 = (bf16[96,768]{1,0:T(8,128)(2,1)S(1)}, bf16[96,768]{1,0:T(8,128)(2,1)S(1)}, u32[]{:S(2)}, u32[]{:S(2)}) collective-permute-start(bf16[96,768]{1,0:T(8,128)(2,1)S(1)} %get-tuple-element.117), channel_id=1, source_target_pairs={{0,16},{2,18},{4,20},{6,22},{8,24},{10,26},{12,28},{14,30},{16,0},... | collective-permute-start | bytes 442376 | tf_op jit(solution)/shard_map/ppermute | solution.py:595
  234.4 4.2 %collective-permute-done.24.refs_2_.refs_3_ = bf16[192,768]{1,0:T(8,128)(2,1)S(1)} collective-permute-done((bf16[192,768]{1,0:T(8,128)(2,1)S(1)}, bf16[192,768]{1,0:T(8,128)(2,1)S(1)}, u32[]{:S(2)}, u32[]{:S(2)}) %collective-permute-start.24) | collective-permute-done | bytes 294944 | tf_op jit(solution)/shard_map/ppermute | solution.py:595
  238.6 5.5 %table_grad.1.refs_4_ = f32[1920,384]{1,0:T(8,128)} custom-call(f32[4,512]{1,0:T(4,128)S(1)} %reshape.175.refs_9_.refs_0_, bf16[2048,384]{1,0:T(8,128)(2,1)S(1)} %bitcast.37, bf16[96,768]{1,0:T(8,128)(2,1)S(1)} %get-tuple-element.112.refs_2_), custom_call_target="tpu_custom_call" | custom-call | bytes 5500 | tf_op jit(solution)/shard_map/table_grad/pallas_call | solution.py:54
  251.0 5.8 %collective-permute-done.27 = bf16[48,3200]{1,0:T(8,128)(2,1)S(1)} collective-permute-done((bf16[48,3200]{1,0:T(8,128)(2,1)S(1)}, bf16[48,3200]{1,0:T(8,128)(2,1)S(1)}, u32[]{:S(2)}, u32[]{:S(2)}) %collective-permute-start.27) | collective-permute-done | bytes 307232 | tf_op jit(solution)/shard_map/ppermute | solution.py:595
  258.8 4.9 %collective-permute-done.28 = bf16[24,3200]{1,0:T(8,128)(2,1)S(1)} collective-permute-done((bf16[24,3200]{1,0:T(8,128)(2,1)S(1)}, bf16[24,3200]{1,0:T(8,128)(2,1)S(1)}, u32[]{:S(2)}, u32[]{:S(2)}) %collective-permute-start.28) | collective-permute-done | bytes 153632 | tf_op jit(solution)/shard_map/ppermute | solution.py:595
  (197 shorter events, 92.9 us)
Async XLA Ops:
  2.9 4.4 %collective-permute-start.1 = (s32[1,1024]{1,0:T(1,128)S(1)}, s32[1,1024]{1,0:T(1,128)S(1)}, u32[]{:S(2)}, u32[]{:S(2)}) collective-permute-start(s32[1,1024]{1,0:T(1,128)S(1)} %pad_add_fusion.1), channel_id=1, source_target_pairs={{0,2},{2,0},{4,6},{6,4},{8,10},{10,8},{12,14},{14,12},{16,18},{18,... | collective-permute-start | bytes 12296 | tf_op jit(solution)/shard_map/ppermute | solution.py:595
  7.2 4.5 %collective-permute-start.3 = (s32[1,1024]{1,0:T(1,128)S(1)}, s32[1,1024]{1,0:T(1,128)S(1)}, u32[]{:S(2)}, u32[]{:S(2)}) collective-permute-start(s32[1,1024]{1,0:T(1,128)S(1)} %pad_add_fusion.1), channel_id=1, source_target_pairs={{0,6},{2,4},{4,2},{6,0},{8,14},{10,12},{12,10},{14,8},{16,22},{18,... | collective-permute-start | bytes 12296 | tf_op jit(solution)/shard_map/ppermute | solution.py:595
  12.4 4.5 %collective-permute-start.4 = (s32[4,1024]{1,0:T(4,128)S(1)}, s32[4,1024]{1,0:T(4,128)S(1)}, u32[]{:S(2)}, u32[]{:S(2)}) collective-permute-start(s32[4,1024]{1,0:T(4,128)S(1)} %pad_add_fusion), channel_id=1, source_target_pairs={{0,8},{2,10},{4,12},{6,14},{8,0},{10,2},{12,4},{14,6},{16,24},{18,... | collective-permute-start | bytes 49160 | tf_op jit(solution)/shard_map/ppermute | solution.py:595
  14.1 4.7 %collective-permute-start.5 = (s32[4,1024]{1,0:T(4,128)S(1)}, s32[4,1024]{1,0:T(4,128)S(1)}, u32[]{:S(2)}, u32[]{:S(2)}) collective-permute-start(s32[4,1024]{1,0:T(4,128)S(1)} %pad_add_fusion), channel_id=1, source_target_pairs={{0,16},{2,18},{4,20},{6,22},{8,24},{10,26},{12,28},{14,30},{16,0},... | collective-permute-start | bytes 49160 | tf_op jit(solution)/shard_map/ppermute | solution.py:595
  16.7 5.5 %collective-permute-start.6 = (s32[4,1024]{1,0:T(4,128)S(1)}, s32[4,1024]{1,0:T(4,128)S(1)}, u32[]{:S(2)}, u32[]{:S(2)}) collective-permute-start(s32[4,1024]{1,0:T(4,128)S(1)} %pad_add_fusion), channel_id=1, source_target_pairs={{0,24},{2,26},{4,28},{6,30},{8,16},{10,18},{12,20},{14,22},{16,8},... | collective-permute-start | bytes 49160 | tf_op jit(solution)/shard_map/ppermute | solution.py:595
  34.0 36.4 %all-to-all-start = ((bf16[16,128,384]{2,1,0:T(8,128)(2,1)}), bf16[16,128,384]{2,1,0:T(8,128)(2,1)}, u32[]{:S(2)}, u32[]{:S(2)}) async-start(bf16[16,128,384]{2,1,0:T(8,128)(2,1)} %bitcast.3), calls=%async_computation | async-start | bytes 3145728 | tf_op jit(solution)/shard_map/all_to_all | solution.py:692
  38.8 30.6 %collective-permute-start.7 = (bf16[3,768,384]{2,1,0:T(8,128)(2,1)S(1)}, bf16[3,768,384]{2,1,0:T(8,128)(2,1)S(1)}, u32[]{:S(2)}, u32[]{:S(2)}) collective-permute-start(bf16[3,768,384]{2,1,0:T(8,128)(2,1)S(1)} %copy-done.3), channel_id=1, source_target_pairs={{0,1},{1,0},{2,3},{3,2},{4,5},{5,4},{6,7},{7,6},{8,9},{9,8},{10,11... | collective-permute-start | bytes 5308424 | tf_op jit(solution)/shard_map/ppermute | solution.py:591
  117.3 10.5 %collective-permute-start.9 = (bf16[512,1536]{1,0:T(8,128)(2,1)}, bf16[512,1536]{1,0:T(8,128)(2,1)S(1)}, u32[]{:S(2)}, u32[]{:S(2)}) collective-permute-start(bf16[512,1536]{1,0:T(8,128)(2,1)} %get-tuple-element.81), channel_id=1, source_target_pairs={{0,1},{1,0},{2,3},{3,2},{4,5},{5,4},{6,7},{7,6},{8,9},{9,8},{10,11... | collective-permute-start | bytes 4718600 | tf_op jit(solution)/shard_map/ppermute | solution.py:591
  123.2 15.9 %collective-permute-start.11 = (bf16[512,1536]{1,0:T(8,128)(2,1)S(1)}, bf16[512,1536]{1,0:T(8,128)(2,1)S(1)}, u32[]{:S(2)}, u32[]{:S(2)}) collective-permute-start(bf16[512,1536]{1,0:T(8,128)(2,1)S(1)} %get-tuple-element.87), channel_id=1, source_target_pairs={{0,1},{1,0},{2,3},{3,2},{4,5},{5,4},{6,7},{7,6},{8,9},{9,8},{10,11... | collective-permute-start | bytes 4718600 | tf_op jit(solution)/shard_map/ppermute | solution.py:591
  123.8 15.3 %collective-permute-start.12 = (bf16[512,768]{1,0:T(8,128)(2,1)S(1)}, bf16[512,768]{1,0:T(8,128)(2,1)S(1)}, u32[]{:S(2)}, u32[]{:S(2)}) collective-permute-start(bf16[512,768]{1,0:T(8,128)(2,1)S(1)} %get-tuple-element.88.refs_2_), channel_id=1, source_target_pairs={{0,1},{1,0},{2,3},{3,2},{4,5},{5,4},{6,7},{7,6},{8,9},{9,8},{10,11... | collective-permute-start | bytes 2359304 | tf_op jit(solution)/shard_map/ppermute | solution.py:591
  130.5 21.1 %collective-permute-start.13 = (bf16[768,768]{1,0:T(8,128)(2,1)S(1)}, bf16[768,768]{1,0:T(8,128)(2,1)}, u32[]{:S(2)}, u32[]{:S(2)}) collective-permute-start(bf16[768,768]{1,0:T(8,128)(2,1)S(1)} %get-tuple-element.91), channel_id=1, source_target_pairs={{0,2},{1,5},{2,0},{3,7},{4,6},{5,1},{6,4},{7,3},{8,10},{9,13},{10,... | collective-permute-start | bytes 3538952 | tf_op jit(solution)/shard_map/ppermute | solution.py:601
  141.8 25.0 %collective-permute-start.15 = (bf16[768,768]{1,0:T(8,128)(2,1)S(1)}, bf16[768,768]{1,0:T(8,128)(2,1)S(1)}, u32[]{:S(2)}, u32[]{:S(2)}) collective-permute-start(bf16[768,768]{1,0:T(8,128)(2,1)S(1)} %get-tuple-element.95), channel_id=1, source_target_pairs={{0,2},{1,5},{2,0},{3,7},{4,6},{5,1},{6,4},{7,3},{8,10},{9,13},{10,... | collective-permute-start | bytes 3538952 | tf_op jit(solution)/shard_map/ppermute | solution.py:601
  153.0 13.1 %collective-permute-start.16 = (bf16[384,768]{1,0:T(8,128)(2,1)S(1)}, bf16[384,768]{1,0:T(8,128)(2,1)S(1)}, u32[]{:S(2)}, u32[]{:S(2)}) collective-permute-start(bf16[384,768]{1,0:T(8,128)(2,1)S(1)} %get-tuple-element.96), channel_id=1, source_target_pairs={{0,4},{1,3},{2,6},{3,1},{4,0},{5,7},{6,2},{7,5},{8,12},{9,11},{10,... | collective-permute-start | bytes 1769480 | tf_op jit(solution)/shard_map/ppermute | solution.py:601
  164.4 18.8 %collective-permute-start.20 = (bf16[3,512,384]{2,1,0:T(8,128)(2,1)}, bf16[3,512,384]{2,1,0:T(8,128)(2,1)}, u32[]{:S(2)}, u32[]{:S(2)}) collective-permute-start(bf16[3,512,384]{2,1,0:T(8,128)(2,1)} %get-tuple-element.102), channel_id=1, source_target_pairs={{0,1},{1,0},{2,3},{3,2},{4,5},{5,4},{6,7},{7,6},{8,9},{9,8},{10,11... | collective-permute-start | bytes 3538952 | tf_op jit(solution)/shard_map/ppermute | solution.py:591
  171.5 67.1 %all-to-all-start.1 = ((bf16[16,128,384]{2,1,0:T(8,128)(2,1)}), bf16[16,128,384]{2,1,0:T(8,128)(2,1)S(1)}, u32[]{:S(2)}, u32[]{:S(2)}) async-start(bf16[16,128,384]{2,1,0:T(8,128)(2,1)} %bitcast.14), calls=%async_computation.1 | async-start | bytes 3145728 | tf_op jit(solution)/shard_map/all_to_all | solution.py:741
  194.3 33.2 %collective-permute-start.25 = (bf16[192,3200]{1,0:T(8,128)(2,1)S(1)}, bf16[192,3200]{1,0:T(8,128)(2,1)S(1)}, u32[]{:S(2)}, u32[]{:S(2)}) collective-permute-start(bf16[192,3200]{1,0:T(8,128)(2,1)S(1)} %get-tuple-element.110), channel_id=1, source_target_pairs={{0,2},{1,5},{2,0},{3,7},{4,6},{5,1},{6,4},{7,3},{8,10},{9,13},{10,... | collective-permute-start | bytes 3686408 | tf_op jit(solution)/shard_map/ppermute | solution.py:601
  196.3 20.8 %collective-permute-start.17 = (bf16[384,768]{1,0:T(8,128)(2,1)S(1)}, bf16[384,768]{1,0:T(8,128)(2,1)S(1)}, u32[]{:S(2)}, u32[]{:S(2)}) collective-permute-start(bf16[384,768]{1,0:T(8,128)(2,1)S(1)} %copy-done.37), channel_id=1, source_target_pairs={{0,4},{1,3},{2,6},{3,1},{4,0},{5,7},{6,2},{7,5},{8,12},{9,11},{10,... | collective-permute-start | bytes 1769480 | tf_op jit(solution)/shard_map/ppermute | solution.py:601
  197.8 15.0 %collective-permute-start.18 = (bf16[192,768]{1,0:T(8,128)(2,1)S(1)}, bf16[192,768]{1,0:T(8,128)(2,1)S(1)}, u32[]{:S(2)}, u32[]{:S(2)}) collective-permute-start(bf16[192,768]{1,0:T(8,128)(2,1)S(1)} %copy-done.39), channel_id=1, source_target_pairs={{0,8},{2,10},{4,12},{6,14},{8,0},{10,2},{12,4},{14,6},{16,24},{18,... | collective-permute-start | bytes 884744 | tf_op jit(solution)/shard_map/ppermute | solution.py:595
  228.5 15.7 %collective-permute-start.26 = (bf16[96,3200]{1,0:T(8,128)(2,1)}, bf16[96,3200]{1,0:T(8,128)(2,1)S(1)}, u32[]{:S(2)}, u32[]{:S(2)}) collective-permute-start(bf16[96,3200]{1,0:T(8,128)(2,1)} %get-tuple-element.113), channel_id=1, source_target_pairs={{0,4},{1,3},{2,6},{3,1},{4,0},{5,7},{6,2},{7,5},{8,12},{9,11},{10,... | collective-permute-start | bytes 1843208 | tf_op jit(solution)/shard_map/ppermute | solution.py:601
  228.5 10.1 %collective-permute-start.24 = (bf16[192,768]{1,0:T(8,128)(2,1)S(1)}, bf16[192,768]{1,0:T(8,128)(2,1)S(1)}, u32[]{:S(2)}, u32[]{:S(2)}) collective-permute-start(bf16[192,768]{1,0:T(8,128)(2,1)S(1)} %get-tuple-element.109), channel_id=1, source_target_pairs={{0,8},{2,10},{4,12},{6,14},{8,0},{10,2},{12,4},{14,6},{16,24},{18,... | collective-permute-start | bytes 884744 | tf_op jit(solution)/shard_map/ppermute | solution.py:595
  229.5 20.7 %collective-permute-start.30 = (bf16[96,768]{1,0:T(8,128)(2,1)S(1)}, bf16[96,768]{1,0:T(8,128)(2,1)S(1)}, u32[]{:S(2)}, u32[]{:S(2)}) collective-permute-start(bf16[96,768]{1,0:T(8,128)(2,1)S(1)} %get-tuple-element.117), channel_id=1, source_target_pairs={{0,16},{2,18},{4,20},{6,22},{8,24},{10,26},{12,28},{14,30},{16,0},... | collective-permute-start | bytes 442376 | tf_op jit(solution)/shard_map/ppermute | solution.py:595
  246.1 10.7 %collective-permute-start.27 = (bf16[48,3200]{1,0:T(8,128)(2,1)S(1)}, bf16[48,3200]{1,0:T(8,128)(2,1)S(1)}, u32[]{:S(2)}, u32[]{:S(2)}) collective-permute-start(bf16[48,3200]{1,0:T(8,128)(2,1)S(1)} %get-tuple-element.115), channel_id=1, source_target_pairs={{0,8},{2,10},{4,12},{6,14},{8,0},{10,2},{12,4},{14,6},{16,24},{18,... | collective-permute-start | bytes 921608 | tf_op jit(solution)/shard_map/ppermute | solution.py:595
  247.6 10.4 %collective-permute-start.29 = (bf16[96,768]{1,0:T(8,128)(2,1)S(1)}, bf16[96,768]{1,0:T(8,128)(2,1)S(1)}, u32[]{:S(2)}, u32[]{:S(2)}) collective-permute-start(bf16[96,768]{1,0:T(8,128)(2,1)S(1)} %get-tuple-element.116), channel_id=1, source_target_pairs={{0,16},{2,18},{4,20},{6,22},{8,24},{10,26},{12,28},{14,30},{16,0},... | collective-permute-start | bytes 442376 | tf_op jit(solution)/shard_map/ppermute | solution.py:595
  256.8 6.8 %collective-permute-start.28 = (bf16[24,3200]{1,0:T(8,128)(2,1)S(1)}, bf16[24,3200]{1,0:T(8,128)(2,1)S(1)}, u32[]{:S(2)}, u32[]{:S(2)}) collective-permute-start(bf16[24,3200]{1,0:T(8,128)(2,1)S(1)} %slice.54), channel_id=1, source_target_pairs={{0,16},{2,18},{4,20},{6,22},{8,24},{10,26},{12,28},{14,30},{16,0},... | collective-permute-start | bytes 460808 | tf_op jit(solution)/shard_map/ppermute | solution.py:595
  (55 other events, 284.0 us)
